TPU v7x, 32 devices: a whole 2x2x4 slice. The times are simulated.
32 devices in a mesh: groups: 2 (over x), curve: 16 (over z, y, core).
Axes of the slice: x: 2, y: 2, z: 4, core: 2. Of those that a mesh axis runs over, the one named last changes fastest.
Arguments:
- fine_latent: bfloat16 [65536, 128], P(('groups', 'curve')), parts along dimension 0, may hold values from -6 to 6
- coarse_latent: bfloat16 [32768, 128], P(('groups', 'curve')), parts along dimension 0, may hold values from -6 to 6
- grad_coarse: bfloat16 [32768, 128], P(('groups', 'curve')), parts along dimension 0, may hold values from -6 to 6
- restrict_weights: bfloat16 [2, 32768], P(None, ('groups', 'curve')), parts along dimension 1, may hold values from 0.25 to 1
- send_rows: int32 [65536], P(('groups', 'curve')), parts along dimension 0, may hold values from 0 to 1024, as said below
- pair_slots: int32 [32768], P(('groups', 'curve')), parts along dimension 0, may hold values from 0 to 2047, as said below
- edge_receivers: int32 [196608], P(('groups', 'curve')), parts along dimension 0, may hold values from 0 to 2047
- edge_offsets: int32 [196608], P(('groups', 'curve')), parts along dimension 0, may hold values from -256 to 256
- edge_weight: bfloat16 [256, 128], replicated, may hold values from -0.375 to 0.375
- node_weight_in: bfloat16 [128, 128], replicated, may hold values from -0.5 to 0.5
- node_weight_out: bfloat16 [128, 128], replicated, may hold values from -0.5 to 0.5
- node_gain: float32 [128], replicated, may hold values from 0.5 to 2
Outputs:
- grad_fine: bfloat16 [65536, 128], P(('groups', 'curve')), parts along dimension 0
- grad_edge: float32 [512, 128], P('groups'), parts along dimension 0
- grad_node_in: float32 [256, 128], P('groups'), parts along dimension 0
- grad_node_out: float32 [256, 128], P('groups'), parts along dimension 0
- grad_gain: float32 [256], P('groups'), parts along dimension 0
There are 2 independent parts, one for each index of `groups`. A program takes and returns all parts, laid end to end along the dimension named above; an argument that names none is the same for every part. Nothing has to cross between parts.
Inputs may be any that keep to these rules, and one draw needn't show every extreme that they name: `send_rows`: in coarse shard d's block, entry s * 128 + t is the local coarse row sent in slot t toward fine shard s, and 1024 marks an empty slot. Every local coarse row is sent once; used slots toward a shard come first; some pair of shards fills all 128 slots. The numbers of used slots from one coarse shard toward the fine shards form the same multiset for every coarse shard, and toward one fine shard from the coarse shards the same multiset again. `pair_slots`: pair k of fine shard s (its fine rows 2 k and 2 k + 1) receives from slot d * 128 + t of coarse shard d's block toward s, the slot that holds its coarse node; each used slot serves exactly one pair.
All inputs are finite; a program needn't handle non-finite values.
Results may differ from a plain program's by a relative error of at most 0.0062.
The roundings to bfloat16 on the way count: a program that leaves them out, or rounds other values in their place, can miss the bound.
Values may be sent and summed in bfloat16 or wider, within the bound.
No kernel may reach another device: no remote copies, remote signals or barrier semaphores. Data moves between devices by JAX's collectives and lax.ppermute only.
A program may use at most 64 MiB of HBM per device.

v0:
```python
import functools
import math

import jax
import jax.numpy as jnp
from jax import lax
from jax.experimental import pallas as pl
from jax.experimental.pallas import tpu as pltpu
from jax.sharding import PartitionSpec as P

HB = 256
LANES = 128
SPAN = 256
EXTRA = 16
TILE = 512
SENDERS = 3

F32 = jnp.float32
BF16 = jnp.bfloat16
NT = (((1,), (1,)), ((), ()))
TN = (((0,), (0,)), ((), ()))


def dot(left, right, dims=(((1,), (0,)), ((), ()))):
    return lax.dot_general(left, right, dims, preferred_element_type=F32)


def silu_slope(values):
    sigm = jax.nn.sigmoid(values)
    return sigm * (1.0 + values * (1.0 - sigm))


def columns(row):
    return jnp.broadcast_to(row, (LANES, LANES)).T


def index_columns(ref, first, count):
    return jnp.concatenate([columns(ref[pl.ds(first + i, 1), :]) for i in range(count)], axis=0)


def small(values):
    return values.astype(F32).astype(BF16)


def place_hot(cols):
    place = small(cols & (SPAN - 1))
    lane = lax.broadcasted_iota(jnp.int32, place.shape, 1)
    one, zero = jnp.ones((), BF16), jnp.zeros((), BF16)
    return jnp.concatenate(
        [jnp.where(place == small(lane + start), one, zero) for start in range(0, SPAN, LANES)],
        axis=1,
    )


def gather_rows(cols, table, width):
    hot = place_hot(cols)
    block = cols // SPAN
    total = table.shape[1]
    step = max(width, 2 * LANES)
    found = [jnp.zeros(cols.shape, F32) for _ in range(width // LANES)]
    for start in range(0, total, step):
        part = dot(hot, table[:, start : start + step])
        for inner in range(0, step, width):
            here = block == (start + inner) // width
            for i in range(len(found)):
                at = inner + i * LANES
                found[i] = jnp.where(here, part[:, at : at + LANES], found[i])
    return found


def two_parts(values):
    high = values.astype(BF16)
    return high, (values - high.astype(F32)).astype(BF16)


def back(values, weight):
    high, low = two_parts(values)
    return dot(high, weight, NT) + dot(low, weight, NT)


def outer(rows, values):
    high, low = two_parts(values)
    both = dot(rows, jnp.concatenate([high, low], axis=1), TN)
    return both[:, 0:LANES] + both[:, LANES:]


def reversed_bits(number, limit):
    result = 0
    while limit > 1:
        result = 2 * result + number % 2
        number //= 2
        limit //= 2
    return result


def fetch(sources, targets, arrivals):
    copies = [
        pltpu.make_async_copy(source, target, arrivals.at[i])
        for i, (source, target) in enumerate(zip(sources, targets))
    ]
    for copy in copies:
        copy.start()
    return copies


def coarse_kernel(
    peers,
    latent_ref,
    grad_ref,
    weights_ref,
    rows_ref,
    w_in_ref,
    w_out_ref,
    gain_ref,
    sent_ref,
    table_ref,
    *held,
):
    *held, arrivals = held
    sources = (latent_ref, grad_ref, weights_ref, rows_ref, w_in_ref, w_out_ref, gain_ref)
    copies = fetch(sources, held, arrivals)
    for copy in copies:
        copy.wait()
    latent_ref, grad_ref, weights_ref, rows_ref, w_in_ref, w_out_ref, gain_ref = held
    count = latent_ref.shape[0]
    chunk = SPAN // peers
    capacity = sent_ref.shape[1] - EXTRA - max(EXTRA, chunk)
    w_in, w_out, gain = w_in_ref[...], w_out_ref[...], gain_ref[...]
    term_in = jnp.zeros((LANES, LANES), F32)
    term_out = jnp.zeros((LANES, LANES), F32)
    term_gain = jnp.zeros((1, LANES), F32)
    for block in range(count // SPAN):
        rows = pl.ds(block * SPAN, SPAN)
        latent = latent_ref[rows, :]
        pre = dot(latent, w_in)
        sigm = jax.nn.sigmoid(pre)
        hidden = (pre * sigm).astype(BF16)
        slope = sigm * (1.0 + pre * (1.0 - sigm))
        mapped = dot(hidden, w_out)
        centred = mapped - jnp.mean(mapped, axis=1, keepdims=True)
        inverse = lax.rsqrt(jnp.mean(centred * centred, axis=1, keepdims=True) + 1e-05)
        normed = centred * inverse
        upstream = grad_ref[rows, :].astype(F32)
        scaled = upstream * gain
        grad_mapped = (
            inverse
            * (
                scaled
                - jnp.mean(scaled, axis=1, keepdims=True)
                - normed * jnp.mean(scaled * normed, axis=1, keepdims=True)
            )
        ).astype(BF16)
        grad_pre = (dot(grad_mapped, w_out, NT) * slope).astype(BF16)
        grad_in = (upstream + dot(grad_pre, w_in, NT)).astype(BF16)
        term_gain += jnp.sum(upstream * normed, axis=0, keepdims=True)
        term_in += dot(latent, grad_pre, TN)
        term_out += dot(hidden, grad_mapped, TN)
        table_ref[:, block * SPAN : block * SPAN + LANES] = grad_in
        for half in range(SPAN // LANES):
            at = block * SPAN + half * LANES
            pair = weights_ref[:, at : at + LANES].astype(F32)
            square = jnp.concatenate([pair, jnp.zeros((LANES - 2, LANES), F32)], axis=0)
            table_ref[
                half * LANES : (half + 1) * LANES, block * SPAN + LANES : (block + 1) * SPAN
            ] = square.T.astype(BF16)
    gain_high, gain_low = two_parts(term_gain)
    gain_rows = jnp.concatenate([gain_high.astype(F32), gain_low.astype(F32)], axis=0)
    terms = jnp.concatenate([term_in, term_out], axis=0)
    per_step = 256 // LANES
    for first in range(0, rows_ref.shape[0], per_step):
        cols = index_columns(rows_ref, first, per_step)
        sent, weight = gather_rows(cols, table_ref[...], SPAN)
        for part in range(per_step * LANES // capacity):
            peer = first * LANES // capacity + part
            rows = slice(part * capacity, (part + 1) * capacity)
            sent_ref[peer, 0:capacity, :] = sent[rows].astype(BF16)
            square = weight[rows]
            if capacity < LANES:
                square = jnp.concatenate(
                    [square, jnp.zeros((LANES - capacity, LANES), F32)], axis=0
                )
            extra = jnp.concatenate(
                [square.T[0:2], gain_rows, jnp.zeros((EXTRA - 4, LANES), F32)], axis=0
            )
            sent_ref[peer, capacity : capacity + EXTRA, :] = extra.astype(BF16)
            first_row = reversed_bits(peer, peers) * chunk
            share = terms[first_row : first_row + chunk]
            if chunk < EXTRA:
                share = jnp.concatenate([share, jnp.zeros((EXTRA - chunk, LANES), F32)], axis=0)
            sent_ref[peer, capacity + EXTRA :, :] = share.astype(BF16)


def order_edges(recv_ref, off_ref, ordered, stats_vmem, wide, counts, fine_count):
    rows = recv_ref.shape[0]
    shift = (fine_count // LANES).bit_length() - 1
    lane = lax.broadcasted_iota(jnp.int32, (LANES, LANES), 1)
    sub = lax.broadcasted_iota(jnp.int32, (LANES, LANES), 0)
    group = 4
    counts[...] = jnp.zeros(counts.shape, F32)

    def count(step, carry):
        for i in range(group):
            row = step * group + i
            recv = columns(recv_ref[pl.ds(row, 1), :])
            wide[pl.ds(row * LANES, LANES), :] = recv
            hot = jnp.where((recv >> shift) == lane, 1.0, 0.0)
            counts[pl.ds(row, 1), :] = jnp.sum(hot, axis=0, keepdims=True)
        return carry

    lax.fori_loop(0, rows // group, count, 0)
    number = counts[...]
    before_row = jnp.where(lane < sub, 1.0, 0.0).astype(BF16)
    before_bucket = jnp.where(sub < lane, 1.0, 0.0).astype(BF16)
    total = jnp.broadcast_to(jnp.sum(number, axis=0, keepdims=True), (8, LANES))
    high = jnp.floor(total * (1.0 / 64.0))
    low = total - 64.0 * high
    start = 64.0 * dot(high.astype(BF16), before_bucket) + dot(low.astype(BF16), before_bucket)
    counts[...] = dot(before_row, number.astype(BF16)) + start[0:1]
    lane_place = small(lane)
    zero = jnp.zeros((), BF16)

    def place(step, moved):
        left, right = [], []
        for i in range(group):
            row = step * group + i
            recv = wide[pl.ds(row * LANES, LANES), :]
            off = columns(off_ref[pl.ds(row, 1), :]) + HB
            bucket = recv >> shift
            same = (bucket == (recv_ref[pl.ds(row, 1), :] >> shift)) & (lane < sub)
            mine = jnp.where(bucket == lane, counts[pl.ds(row, 1), :], 0.0)
            position = jnp.sum(mine + jnp.where(same, 1.0, 0.0), axis=1, keepdims=True)
            position = jnp.broadcast_to(position, (LANES, LANES)).astype(jnp.int32)
            here = (position >> 7) == (lane & 63)
            both = jnp.where(lane < 64, recv & 255, off & 255)
            rest = ((recv >> 8) << 2) | (off >> 8)
            first = small(jnp.where(here, both, 0))
            second = small(jnp.where(here & (lane < 64), rest, 0))
            left.append(jnp.concatenate([first, second], axis=1))
            right.append(
                jnp.where(small(position & 127) == lane_place, jnp.ones((), BF16), zero)
            )
        return moved + dot(jnp.concatenate(left, axis=0), jnp.concatenate(right, axis=0), TN)

    moved = lax.fori_loop(0, rows // group, place, jnp.zeros((2 * LANES, LANES), F32))
    moved = moved.astype(jnp.int32)
    rest = moved[LANES : LANES + rows]
    recv = moved[0:rows] + ((rest >> 2) << 8)
    send = recv + moved[64 : 64 + rows] + ((rest & 3) << 8)
    ordered[0] = recv
    ordered[1] = send
    lane = lax.broadcasted_iota(jnp.int32, (rows, LANES), 1)
    recv, send = recv.astype(F32), send.astype(F32)
    stats = jnp.where(
        lane < 2,
        jnp.where(
            lane == 0,
            jnp.min(recv, axis=1, keepdims=True),
            jnp.max(recv, axis=1, keepdims=True),
        ),
        jnp.where(
            lane == 2,
            jnp.min(send, axis=1, keepdims=True),
            jnp.max(send, axis=1, keepdims=True),
        ),
    )
    stats_vmem[...] = stats.astype(jnp.int32)


def tile_bases(stats, tile, fine_count):
    count = TILE // LANES
    rows = [tile * count + i for i in range(count)]

    def extreme(pick, at):
        value = stats[rows[0], at]
        for row in rows[1:]:
            value = pick(value, stats[row, at])
        return value

    recv_base = jnp.minimum((extreme(jnp.minimum, 0) >> 4) << 4, fine_count - SPAN)
    send_base = jnp.minimum(
        (extreme(jnp.minimum, 2) >> 4) << 4, fine_count + 2 * HB - SENDERS * SPAN
    )
    fits = (extreme(jnp.maximum, 1) - recv_base < SPAN) & (
        extreme(jnp.maximum, 3) - send_base < SENDERS * SPAN
    )
    return recv_base, send_base, fits


def either(fits, recv_base, send_base, fine_count, work):
    @pl.when(fits)
    def _():
        work(recv_base, 1, send_base, SENDERS)

    @pl.when(jnp.logical_not(fits))
    def _():
        work(0, fine_count // SPAN, 0, fine_count // SPAN + 2)


def block_rows(base, block):
    return pl.ds(pl.multiple_of(base + block * SPAN, 16), SPAN)


def gather_blocks(cols, table, base, blocks):
    local = cols - base
    hot = place_hot(local)
    block = local >> 8
    found = None
    for start in range(0, blocks, 2):
        some = range(start, min(start + 2, blocks))
        part = dot(hot, jnp.concatenate([table[block_rows(base, j), :] for j in some], axis=1))
        for i, j in enumerate(some):
            one = part[:, i * LANES : (i + 1) * LANES]
            found = one if found is None else jnp.where(block == j, one, found)
    return found


def slope_kernel(
    recv_hbm,
    off_hbm,
    fine_hbm,
    weight_hbm,
    low_hbm,
    high_hbm,
    slope_hbm,
    ordered,
    stats_vmem,
    recv_ref,
    off_ref,
    window,
    weight_ref,
    wide,
    counts,
    slope_ref,
    stats,
    arrivals,
    stats_done,
    leaving,
):
    fine_count = fine_hbm.shape[0]
    copies = fetch(
        (recv_hbm, off_hbm, fine_hbm, weight_hbm, low_hbm, high_hbm),
        (
            recv_ref,
            off_ref,
            window.at[pl.ds(HB, fine_count)],
            weight_ref,
            window.at[pl.ds(0, HB)],
            window.at[pl.ds(HB + fine_count, HB)],
        ),
        arrivals,
    )
    copies[0].wait()
    copies[1].wait()
    order_edges(recv_ref, off_ref, ordered, stats_vmem, wide, counts, fine_count)
    stats_copy = pltpu.make_async_copy(stats_vmem, stats, stats_done)
    stats_copy.start()
    for copy in copies[2:]:
        copy.wait()
    stats_copy.wait()
    count = TILE // LANES
    weight = weight_ref[...]

    def leave(tile):
        rows = pl.ds(pl.multiple_of(tile * TILE, TILE), TILE)
        return pltpu.make_async_copy(slope_ref.at[rows], slope_hbm.at[rows], leaving.at[tile])

    def step(tile, carry):
        recv_base, send_base, fits = tile_bases(stats, tile, fine_count)

        def work(recv_base, recv_blocks, send_base, send_blocks):
            recv = index_columns(ordered.at[0], tile * count, count)
            send = index_columns(ordered.at[1], tile * count, count)
            sender = gather_blocks(send, window, send_base, send_blocks)
            receiver = gather_blocks(recv + HB, window, recv_base + HB, recv_blocks)
            inputs = jnp.concatenate([sender.astype(BF16), receiver.astype(BF16)], axis=1)
            slope_ref[pl.ds(pl.multiple_of(tile * TILE, TILE), TILE), :] = silu_slope(
                dot(inputs, weight)
            )

        either(fits, recv_base, send_base, fine_count, work)
        leave(tile).start()
        return carry

    tiles = slope_ref.shape[0] // TILE
    lax.fori_loop(0, tiles, step, 0)
    for tile in range(tiles):
        leave(tile).wait()


def edge_kernel(
    stats,
    arrived_hbm,
    slots_hbm,
    slope_hbm,
    ordered_hbm,
    low_hbm,
    fine_hbm,
    high_hbm,
    weight_hbm,
    summed_ref,
    to_prev_ref,
    to_next_ref,
    term_ref,
    coarse_ref,
    gain_ref,
    slot_table,
    grad_table,
    grad_rows,
    send_sum,
    recv_sum,
    arrived_ref,
    slots_ref,
    slope_ref,
    ordered,
    window,
    weight_ref,
    arrivals,
):
    fine_count = fine_hbm.shape[0]
    copies = fetch(
        (
            arrived_hbm,
            slots_hbm,
            ordered_hbm,
            slope_hbm,
            fine_hbm,
            low_hbm,
            high_hbm,
            weight_hbm,
        ),
        (
            arrived_ref,
            slots_ref,
            ordered,
            slope_ref,
            window.at[pl.ds(HB, fine_count)],
            window.at[pl.ds(0, HB)],
            window.at[pl.ds(HB + fine_count, HB)],
            weight_ref,
        ),
        arrivals,
    )
    send_sum[...] = jnp.zeros(send_sum.shape, F32)
    recv_sum[...] = jnp.zeros(recv_sum.shape, F32)
    peers = arrived_ref.shape[0]
    share = max(EXTRA, SPAN // peers)
    capacity = arrived_ref.shape[1] - EXTRA - share
    per_block = SPAN // capacity
    copies[0].wait()
    copies[1].wait()
    coarse = jnp.zeros((share, LANES), F32)
    gain = jnp.zeros((1, LANES), F32)
    for peer in range(peers):
        block, part = divmod(peer, per_block)
        rows = slice(part * capacity, (part + 1) * capacity)
        slot_table[rows, block * SPAN : block * SPAN + LANES] = arrived_ref[peer, 0:capacity, :]
        extra = arrived_ref[peer, capacity : capacity + EXTRA, :].astype(F32)
        square = jnp.concatenate([extra, jnp.zeros((LANES - EXTRA, LANES), F32)], axis=0).T
        slot_table[rows, block * SPAN + LANES : (block + 1) * SPAN] = square[0:capacity].astype(
            BF16
        )
        gain += extra[2:3] + extra[3:4]
        coarse += arrived_ref[peer, capacity + EXTRA :, :].astype(F32)
    coarse_ref[...] = coarse.astype(BF16)
    gain_ref[...] = gain

    per_step = SPAN // LANES
    for first in range(0, slots_ref.shape[0], per_step):
        cols = index_columns(slots_ref, first, per_step)
        grad, weight = gather_rows(cols, slot_table, SPAN)
        for r in range(2):
            rows = (grad * weight[:, r : r + 1]).astype(BF16).astype(F32)
            grad_rows[pl.ds(2 * first * LANES + r, SPAN, stride=2), :] = rows
    grad_table[...] = grad_rows[...].astype(BF16)
    for copy in copies[2:]:
        copy.wait()

    count = TILE // LANES
    one, zero = jnp.ones((), BF16), jnp.zeros((), BF16)
    sub = small(lax.broadcasted_iota(jnp.int32, (SPAN, LANES), 0))

    def add_rows(total, base, blocks, at, cols, values):
        hot = []
        for i in range(count):
            row = ordered[at, pl.ds(cols[0] * count + i, 1), :] - base
            hot.append(jnp.where(sub == small(row & (SPAN - 1)), one, zero))
        hot = jnp.concatenate(hot, axis=1)
        if blocks == 1:
            total[block_rows(base, 0), :] += dot(hot, values)
            return
        block = small((cols[1] - base) >> 8)
        for start in range(0, blocks, 2):
            some = range(start, min(start + 2, blocks))
            spread = [jnp.where(block == jnp.full((), j, BF16), values, zero) for j in some]
            part = dot(hot, jnp.concatenate(spread, axis=1))
            for i, j in enumerate(some):
                total[block_rows(base, j), :] += part[:, i * LANES : (i + 1) * LANES]

    def step(tile, carry):
        recv_base, send_base, fits = tile_bases(stats, tile, fine_count)

        def work(recv_base, recv_blocks, send_base, send_blocks):
            recv = index_columns(ordered.at[0], tile * count, count)
            send = index_columns(ordered.at[1], tile * count, count)
            upstream = gather_blocks(recv, grad_table, recv_base, recv_blocks)
            slope = slope_ref[pl.ds(pl.multiple_of(tile * TILE, TILE), TILE), :]
            values = (upstream * slope).astype(BF16)
            add_rows(recv_sum, recv_base, recv_blocks, 0, (tile, recv), values)
            add_rows(send_sum, send_base, send_blocks, 1, (tile, send), values)

        either(fits, recv_base, send_base, fine_count, work)
        return carry

    lax.fori_loop(0, slope_ref.shape[0] // TILE, step, 0)

    weight_send = weight_ref[0:LANES, :]
    weight_recv = weight_ref[LANES:, :]
    to_prev_ref[...] = back(send_sum[0:HB, :], weight_send).astype(BF16)
    to_next_ref[...] = back(send_sum[HB + fine_count :, :], weight_send).astype(BF16)
    term_send = jnp.zeros((LANES, LANES), F32)
    term_recv = jnp.zeros((LANES, LANES), F32)
    for first in range(0, fine_count + 2 * HB, SPAN):
        at = slice(first, first + SPAN)
        term_send += outer(window[at, :], send_sum[at, :])
    for first in range(0, fine_count, SPAN):
        at = slice(first, first + SPAN)
        moved = slice(HB + first, HB + first + SPAN)
        term_recv += outer(window[moved, :], recv_sum[at, :])
        summed_ref[at, :] = (
            grad_rows[at, :]
            + back(send_sum[moved, :], weight_send)
            + back(recv_sum[at, :], weight_recv)
        )
    term_ref[0:LANES, :] = term_send
    term_ref[LANES:, :] = term_recv


def pair_exchange(upward, downward, even, peers):
    first = [(i, i ^ 1) for i in range(peers)]
    second = [(i, ((i + 1) ^ 1) - 1) for i in range(1, peers - 1)]
    one = lax.ppermute(jnp.where(even, upward, downward), "curve", first)
    two = lax.ppermute(jnp.where(even, downward, upward), "curve", second)
    return jnp.where(even, two, one), jnp.where(even, one, two)


def joined(later, own, there):
    return jnp.where(
        later, jnp.concatenate([there, own], axis=0), jnp.concatenate([own, there], axis=0)
    )


def reduced(term, coarse, device, peers):
    half = term.shape[0] // 2
    odd = (device & 1) == 1
    low, high = term[:half], term[half:]
    gift = jnp.where(odd, low, high).astype(BF16)
    own = jnp.where(odd, high, low) + lax.ppermute(
        gift, "curve", [(i, i ^ 1) for i in range(peers)]
    ).astype(F32)
    hops = peers // 2
    while hops > 1:
        rounded = own.astype(BF16)
        there = lax.ppermute(
            jnp.concatenate([rounded, coarse], axis=0),
            "curve",
            [(i, i ^ hops) for i in range(peers)],
        )
        own = rounded.astype(F32) + there[:half].astype(F32)
        coarse = joined((device & hops) != 0, coarse, there[half:])
        hops //= 2
    coarse = coarse.astype(F32)
    there = lax.ppermute(
        jnp.concatenate([own, coarse], axis=0), "curve", [(i, i ^ 1) for i in range(peers)]
    )
    return joined(odd, own, there[:half]), joined(odd, coarse, there[half:])


def per_device(
    fine_latent,
    coarse_latent,
    grad_coarse,
    restrict_weights,
    send_rows,
    pair_slots,
    edge_receivers,
    edge_offsets,
    edge_weight,
    node_weight_in,
    node_weight_out,
    node_gain,
):
    peers = lax.axis_size("curve")
    device = lax.axis_index("curve")
    even = (device & 1) == 0
    coarse_count = coarse_latent.shape[0]
    fine_count = fine_latent.shape[0]
    edge_count = edge_receivers.shape[0]
    capacity = send_rows.shape[0] // peers
    chunk = SPAN // peers
    share = max(EXTRA, chunk)
    payload = capacity + EXTRA + share
    edge_rows = edge_count // LANES
    window_count = fine_count + 2 * HB
    params = pltpu.CompilerParams(vmem_limit_bytes=64 * 1024 * 1024 - 256 * 1024)
    anywhere = pl.BlockSpec(memory_space=pl.ANY)

    low, high = pair_exchange(fine_latent[fine_count - HB :], fine_latent[:HB], even, peers)

    sent = pl.pallas_call(
        functools.partial(coarse_kernel, peers),
        out_shape=jax.ShapeDtypeStruct((peers, payload, LANES), BF16),
        in_specs=[anywhere] * 7,
        scratch_shapes=[
            pltpu.VMEM((SPAN, coarse_count), BF16),
            pltpu.VMEM((coarse_count, LANES), BF16),
            pltpu.VMEM((coarse_count, LANES), BF16),
            pltpu.VMEM((2, coarse_count), BF16),
            pltpu.VMEM((peers * capacity // LANES, LANES), jnp.int32),
            pltpu.VMEM((LANES, LANES), BF16),
            pltpu.VMEM((LANES, LANES), BF16),
            pltpu.VMEM((1, LANES), F32),
            pltpu.SemaphoreType.DMA((7,)),
        ],
        compiler_params=params,
        cost_estimate=pl.CostEstimate(
            flops=2_000_000_000, bytes_accessed=2_000_000, transcendentals=400_000
        ),
        name="coarse_block",
    )(
        coarse_latent,
        grad_coarse,
        restrict_weights,
        send_rows.reshape(-1, LANES),
        node_weight_in,
        node_weight_out,
        node_gain.reshape(1, LANES),
    )
    arrived = lax.all_to_all(sent, "curve", split_axis=0, concat_axis=0, tiled=True)

    slope, ordered, stats = pl.pallas_call(
        slope_kernel,
        out_shape=(
            jax.ShapeDtypeStruct((edge_count, LANES), F32),
            jax.ShapeDtypeStruct((2, edge_rows, LANES), jnp.int32),
            jax.ShapeDtypeStruct((edge_rows, LANES), jnp.int32),
        ),
        in_specs=[anywhere] * 6,
        out_specs=(
            anywhere,
            pl.BlockSpec(memory_space=pltpu.VMEM),
            pl.BlockSpec(memory_space=pltpu.VMEM),
        ),
        scratch_shapes=[
            pltpu.VMEM((edge_rows, LANES), jnp.int32),
            pltpu.VMEM((edge_rows, LANES), jnp.int32),
            pltpu.VMEM((window_count, LANES), BF16),
            pltpu.VMEM((2 * LANES, LANES), BF16),
            pltpu.VMEM((edge_count, LANES), jnp.int32),
            pltpu.VMEM((LANES, LANES), F32),
            pltpu.VMEM((edge_count, LANES), F32),
            pltpu.SMEM((edge_rows, LANES), jnp.int32),
            pltpu.SemaphoreType.DMA((6,)),
            pltpu.SemaphoreType.DMA,
            pltpu.SemaphoreType.DMA((edge_count // TILE,)),
        ],
        compiler_params=params,
        cost_estimate=pl.CostEstimate(
            flops=16_000_000_000, bytes_accessed=5_000_000, transcendentals=800_000
        ),
        name="edge_slope",
    )(
        edge_receivers.reshape(-1, LANES),
        edge_offsets.reshape(-1, LANES),
        fine_latent,
        edge_weight,
        low,
        high,
    )

    summed, to_prev, to_next, term_edge, coarse_share, term_gain = pl.pallas_call(
        edge_kernel,
        out_shape=(
            jax.ShapeDtypeStruct((fine_count, LANES), F32),
            jax.ShapeDtypeStruct((HB, LANES), BF16),
            jax.ShapeDtypeStruct((HB, LANES), BF16),
            jax.ShapeDtypeStruct((2 * LANES, LANES), F32),
            jax.ShapeDtypeStruct((share, LANES), BF16),
            jax.ShapeDtypeStruct((1, LANES), F32),
        ),
        in_specs=[pl.BlockSpec(memory_space=pltpu.SMEM)] + [anywhere] * 8,
        scratch_shapes=[
            pltpu.VMEM((SPAN, peers * capacity), BF16),
            pltpu.VMEM((fine_count, LANES), BF16),
            pltpu.VMEM((fine_count, LANES), F32),
            pltpu.VMEM((window_count, LANES), F32),
            pltpu.VMEM((fine_count, LANES), F32),
            pltpu.VMEM((peers, payload, LANES), BF16),
            pltpu.VMEM((fine_count // 2 // LANES, LANES), jnp.int32),
            pltpu.VMEM((edge_count, LANES), F32),
            pltpu.VMEM((2, edge_rows, LANES), jnp.int32),
            pltpu.VMEM((window_count, LANES), BF16),
            pltpu.VMEM((2 * LANES, LANES), BF16),
            pltpu.SemaphoreType.DMA((8,)),
        ],
        compiler_params=params,
        cost_estimate=pl.CostEstimate(
            flops=24_000_000_000, bytes_accessed=8_000_000, transcendentals=0
        ),
        name="edge_back",
    )(
        stats,
        arrived,
        pair_slots.reshape(-1, LANES),
        slope,
        ordered,
        low,
        fine_latent,
        high,
        edge_weight,
    )
    edge_terms, coarse_terms = reduced(term_edge, coarse_share[:chunk], device, peers)
    from_prev, from_next = pair_exchange(to_next, to_prev, even, peers)
    coarse_scale = 1.0 / math.sqrt(coarse_count * peers)
    edge_scale = 1.0 / math.sqrt(edge_count * peers)
    grad_fine = jnp.concatenate(
        [
            summed[:HB] + from_prev.astype(F32),
            summed[HB : fine_count - HB],
            summed[fine_count - HB :] + from_next.astype(F32),
        ],
        axis=0,
    ).astype(BF16)
    return (
        grad_fine,
        edge_terms * edge_scale,
        coarse_terms[:LANES] * coarse_scale,
        coarse_terms[LANES:] * coarse_scale,
        term_gain.reshape(LANES) * coarse_scale,
    )


def solution(mesh):
    placed = (
        P(("groups", "curve"), None),
        P(("groups", "curve"), None),
        P(("groups", "curve"), None),
        P(None, ("groups", "curve")),
        P(("groups", "curve")),
        P(("groups", "curve")),
        P(("groups", "curve")),
        P(("groups", "curve")),
        P(),
        P(),
        P(),
        P(),
    )
    return jax.shard_map(
        per_device,
        mesh=mesh,
        in_specs=placed,
        out_specs=(
            P(("groups", "curve"), None),
            P("groups", None),
            P("groups", None),
            P("groups", None),
            P("groups"),
        ),
        check_vma=False,
    )
```

profile of v0, /device:TPU:0, one launch (start us, length us, event | category | flops | bytes accessed | tf_op | source)
XLA Modules:
  0.0 76.3 jit_solution(11478183528241241360)
XLA Ops:
  0.6 1.5 %broadcast_select_fusion.4 = (bf16[256,128]{1,0:T(8,128)(2,1)S(1)}, bf16[256,128]{1,0:T(8,128)(2,1)}) fusion(pred[]{:T(512)S(6)} %eq.6, bf16[2048,128]{1,0:T(8,128)(2,1)} %fine_hbm.3), kind=kLoop, calls=%fused_computation.21 | loop fusion | flops 65536 | bytes 262145 | tf_op jit(solution)/shard_map/jit(_where)/select_n | solution.py:541
  2.8 4.4 %collective-permute-start.1 = (bf16[256,128]{1,0:T(8,128)(2,1)S(1)}, bf16[256,128]{1,0:T(8,128)(2,1)S(1)}, u32[]{:S(2)}, u32[]{:S(2)}) collective-permute-start(bf16[256,128]{1,0:T(8,128)(2,1)S(1)} %get-tuple-element.25), channel_id=1, source_target_pairs={{0,1},{1,0},{2,3},{3,2},{4,5},{5,4},{6,7},{7,6},{8,9},{9,8},{10,11... | collective-permute-start | bytes 196616 | tf_op jit(solution)/shard_map/ppermute | solution.py:541
  7.2 6.4 %coarse_block.1 = bf16[16,160,128]{2,1,0:T(8,128)(2,1)} custom-call(bf16[1024,128]{1,0:T(8,128)(2,1)} %latent_ref.1, bf16[1024,128]{1,0:T(8,128)(2,1)} %grad_ref.1, bf16[2,1024]{1,0:T(2,128)(2,1)} %weights_ref.1, s32[16,128]{1,0:T(8,128)} %bitcast.9, bf16[128,128]{1,0:T(8,128)(2,1)} %w_in_ref.1, bf16[128,128]{1,0:T(8,128)(2,1)} %w_out_ref.1, f32[1,128]{1,0:T(1,128)} %bitcast.11), custom_call_target="tpu_custom_call" | custom-call | flops 2000000000 | bytes 2000000 | tf_op jit(solution)/shard_map/coarse_block/pallas_call | solution.py:609
  13.6 5.0 %all-to-all-start = ((bf16[16,160,128]{2,1,0:T(8,128)(2,1)}), bf16[16,160,128]{2,1,0:T(8,128)(2,1)}, u32[]{:S(2)}, u32[]{:S(2)}) async-start(bf16[16,160,128]{2,1,0:T(8,128)(2,1)} %coarse_block.1), calls=%async_computation | async-start | bytes 1310720 | tf_op jit(solution)/shard_map/all_to_all | solution.py:638
  18.7 0.7 broadcast_select_fusion.2
  19.3 19.3 %edge_slope.1 = (f32[6144,128]{1,0:T(8,128)}, s32[2,48,128]{2,1,0:T(8,128)}, s32[48,128]{1,0:T(8,128)}) custom-call(s32[48,128]{1,0:T(8,128)} %bitcast.7, s32[48,128]{1,0:T(8,128)} %bitcast.8, bf16[2048,128]{1,0:T(8,128)(2,1)} %fine_hbm.3, bf16[256,128]{1,0:T(8,128)(2,1)} %weight_hbm.3, bf16[256,128]{1,0:T(8,128)(2,1)} %get-tuple-element.34.low_hbm, ...), custom_call_target="tpu_custom_call" | custom-call | flops 16000000000 | bytes 5000000 | tf_op jit(solution)/shard_map/edge_slope/pallas_call | solution.py:640
  38.7 14.8 %edge_back.1 = (f32[2048,128]{1,0:T(8,128)}, bf16[256,128]{1,0:T(8,128)(2,1)}, bf16[256,128]{1,0:T(8,128)(2,1)}, f32[256,128]{1,0:T(8,128)}, bf16[16,128]{1,0:T(8,128)(2,1)}, /*index=5*/f32[1,128]{1,0:T(1,128)}) custom-call(s32[48,128]{1,0:T(8,128)} %get-tuple-element.14.stats, bf16[16,160,128]{2,1,0:T(8,128)(2,1)} %all-to-all-done.arrived_hbm, ...), custom_call_target="tpu_custom_call" | custom-call | flops 24000000000 | bytes 8000000 | tf_op jit(solution)/shard_map/edge_back/pallas_call | solution.py:680
  53.4 0.9 %select_convert_fusion = bf16[128,128]{1,0:T(8,128)(2,1)S(1)} fusion(f32[256,128]{1,0:T(8,128)} %get-tuple-element.20, pred[]{:T(512)S(6)} %eq.7), kind=kLoop, calls=%fused_computation.16 | loop fusion | flops 16384 | bytes 98305 | tf_op jit(solution)/shard_map/convert_element_type | solution.py:556
  54.7 0.9 %collective-permute-done.4 = bf16[128,128]{1,0:T(8,128)(2,1)S(1)} collective-permute-done((bf16[128,128]{1,0:T(8,128)(2,1)S(1)}, bf16[128,128]{1,0:T(8,128)(2,1)S(1)}, u32[]{:S(2)}, u32[]{:S(2)}) %collective-permute-start.4) | collective-permute-done | bytes 32800 | tf_op jit(solution)/shard_map/ppermute | solution.py:557
  55.6 0.9 %add_convert_fusion.4 = bf16[128,128]{1,0:T(8,128)(2,1)S(1)} fusion(bf16[128,128]{1,0:T(8,128)(2,1)S(1)} %collective-permute-done.4, f32[256,128]{1,0:T(8,128)} %get-tuple-element.20, pred[]{:T(512)S(6)} %eq.7), kind=kLoop, calls=%fused_computation.15 | loop fusion | flops 65536 | bytes 196609 | tf_op jit(solution)/shard_map/convert_element_type | solution.py:562
  56.5 0.7 pad_maximum_fusion.6
  57.2 2.7 %collective-permute-start.5 = (bf16[144,128]{1,0:T(8,128)(2,1)S(1)}, bf16[144,128]{1,0:T(8,128)(2,1)S(1)}, u32[]{:S(2)}, u32[]{:S(2)}) collective-permute-start(bf16[144,128]{1,0:T(8,128)(2,1)S(1)} %pad_maximum_fusion.6), channel_id=1, source_target_pairs={{0,8},{1,9},{2,10},{3,11},{4,12},{5,13},{6,14},{7,15},{8,0},{9,1},... | collective-permute-start | bytes 110600 | tf_op jit(solution)/shard_map/ppermute | solution.py:563
  59.9 0.9 %broadcast_select_fusion.1 = (bf16[256,128]{1,0:T(8,128)(2,1)S(1)}, bf16[256,128]{1,0:T(8,128)(2,1)S(1)}) fusion(bf16[256,128]{1,0:T(8,128)(2,1)} %get-tuple-element.18, bf16[256,128]{1,0:T(8,128)(2,1)} %get-tuple-element.19, pred[]{:T(512)S(6)} %eq.6), kind=kLoop, calls=%fused_computation.18 | loop fusion | flops 65536 | bytes 262145 | tf_op jit(solution)/shard_map/jit(_where)/select_n | solution.py:542
  60.8 0.7 collective-permute-start.2
  61.5 2.9 %collective-permute-start.3 = (bf16[256,128]{1,0:T(8,128)(2,1)S(1)}, bf16[256,128]{1,0:T(8,128)(2,1)S(1)}, u32[]{:S(2)}, u32[]{:S(2)}) collective-permute-start(bf16[256,128]{1,0:T(8,128)(2,1)S(1)} %get-tuple-element.32), channel_id=1, source_target_pairs={{0,1},{1,0},{2,3},{3,2},{4,5},{5,4},{6,7},{7,6},{8,9},{9,8},{10,11... | collective-permute-start | bytes 196616 | tf_op jit(solution)/shard_map/ppermute | solution.py:541
  64.4 0.8 %maximum_select_fusion.2 = bf16[32,128]{1,0:T(8,128)(2,1)S(1)} fusion(bf16[16,128]{1,0:T(8,128)(2,1)} %get-tuple-element.21, bf16[16,128]{1,0:T(8,128)(2,1)S(1)} %slice.71, pred[]{:T(512)S(6)} %ne.9), kind=kLoop, calls=%fused_computation.29 | loop fusion | flops 36864 | bytes 16385 | tf_op jit(solution)/shard_map/jit(_where)/select_n | solution.py:547
  65.2 1.5 %collective-permute-start.6 = (bf16[160,128]{1,0:T(8,128)(2,1)S(1)}, bf16[160,128]{1,0:T(8,128)(2,1)S(1)}, u32[]{:S(2)}, u32[]{:S(2)}) collective-permute-start(bf16[160,128]{1,0:T(8,128)(2,1)S(1)} %pad_maximum_fusion.5), channel_id=1, source_target_pairs={{0,4},{1,5},{2,6},{3,7},{4,0},{5,1},{6,2},{7,3},{8,12},{9,13},{10,... | collective-permute-start | bytes 122888 | tf_op jit(solution)/shard_map/ppermute | solution.py:563
  66.7 1.1 %multiply_bitcast_fusion = f32[128]{0:T(128)} fusion(f32[1,128]{1,0:T(1,128)} %get-tuple-element.22), kind=kLoop, calls=%fused_computation.30 | loop fusion | flops 128 | bytes 1024 | tf_op jit(solution)/shard_map/mul | solution.py:738
  67.9 1.2 %slice.96 = bf16[1536,128]{1,0:T(8,128)(2,1)S(1)} slice(f32[2048,128]{1,0:T(8,128)} %get-tuple-element.17), slice={[256:1792], [0:128]} | slice | bytes 786432 | tf_op jit(solution)/shard_map/slice | solution.py:728
  69.3 1.5 %collective-permute-start.7 = (bf16[192,128]{1,0:T(8,128)(2,1)S(1)}, bf16[192,128]{1,0:T(8,128)(2,1)S(1)}, u32[]{:S(2)}, u32[]{:S(2)}) collective-permute-start(bf16[192,128]{1,0:T(8,128)(2,1)S(1)} %pad_maximum_fusion.4), channel_id=1, source_target_pairs={{0,2},{1,3},{2,0},{3,1},{4,6},{5,7},{6,4},{7,5},{8,10},{9,11},{10,... | collective-permute-start | bytes 147464 | tf_op jit(solution)/shard_map/ppermute | solution.py:563
  70.8 1.0 %add_convert_fusion.1 = (bf16[256,128]{1,0:T(8,128)(2,1)S(1)}, bf16[256,128]{1,0:T(8,128)(2,1)S(1)}) fusion(f32[2048,128]{1,0:T(8,128)} %get-tuple-element.17, bf16[256,128]{1,0:T(8,128)(2,1)S(1)} %collective-permute-done.2, bf16[256,128]{1,0:T(8,128)(2,1)S(1)} %collective-permute-done.3, pred[]{:T(512)S(6)} %eq.6), kind=kLoop, calls=%fused_computation.9 | loop fusion | flops 262144 | bytes 524289 | tf_op jit(solution)/shard_map/convert
  71.9 1.6 %collective-permute-done.7 = bf16[192,128]{1,0:T(8,128)(2,1)S(1)} collective-permute-done((bf16[192,128]{1,0:T(8,128)(2,1)S(1)}, bf16[192,128]{1,0:T(8,128)(2,1)S(1)}, u32[]{:S(2)}, u32[]{:S(2)}) %collective-permute-start.7) | collective-permute-done | bytes 49184 | tf_op jit(solution)/shard_map/ppermute | solution.py:563
  73.6 0.8 %pad_maximum_fusion = bf16[2048,128]{1,0:T(8,128)(2,1)} fusion(bf16[256,128]{1,0:T(8,128)(2,1)S(1)} %get-tuple-element.24, bf16[1536,128]{1,0:T(8,128)(2,1)S(1)} %slice.96, bf16[256,128]{1,0:T(8,128)(2,1)S(1)} %get-tuple-element.23), kind=kLoop, calls=%fused_computation.1 | loop fusion | flops 1572864 | bytes 1048576 | tf_op jit(solution)/shard_map/concatenate | solution.py:725
  74.9 0.7 fusion.1
  (24 shorter events, 2.6 us)
Async XLA Ops:
  2.2 16.5 %collective-permute-start = (bf16[256,128]{1,0:T(8,128)(2,1)}, bf16[256,128]{1,0:T(8,128)(2,1)S(1)}, u32[]{:S(2)}, u32[]{:S(2)}) collective-permute-start(bf16[256,128]{1,0:T(8,128)(2,1)} %get-tuple-element.26), channel_id=1, source_target_pairs={{1,2},{2,1},{3,4},{4,3},{5,6},{6,5},{7,8},{8,7},{9,10},{10,9},{11,... | collective-permute-start | bytes 196616 | tf_op jit(solution)/shard_map/ppermute | solution.py:542
  2.8 15.9 %collective-permute-start.1 = (bf16[256,128]{1,0:T(8,128)(2,1)S(1)}, bf16[256,128]{1,0:T(8,128)(2,1)S(1)}, u32[]{:S(2)}, u32[]{:S(2)}) collective-permute-start(bf16[256,128]{1,0:T(8,128)(2,1)S(1)} %get-tuple-element.25), channel_id=1, source_target_pairs={{0,1},{1,0},{2,3},{3,2},{4,5},{5,4},{6,7},{7,6},{8,9},{9,8},{10,11... | collective-permute-start | bytes 196616 | tf_op jit(solution)/shard_map/ppermute | solution.py:541
  13.6 25.0 %all-to-all-start = ((bf16[16,160,128]{2,1,0:T(8,128)(2,1)}), bf16[16,160,128]{2,1,0:T(8,128)(2,1)}, u32[]{:S(2)}, u32[]{:S(2)}) async-start(bf16[16,160,128]{2,1,0:T(8,128)(2,1)} %coarse_block.1), calls=%async_computation | async-start | bytes 1310720 | tf_op jit(solution)/shard_map/all_to_all | solution.py:638
  54.3 1.3 %collective-permute-start.4 = (bf16[128,128]{1,0:T(8,128)(2,1)S(1)}, bf16[128,128]{1,0:T(8,128)(2,1)S(1)}, u32[]{:S(2)}, u32[]{:S(2)}) collective-permute-start(bf16[128,128]{1,0:T(8,128)(2,1)S(1)} %select_convert_fusion), channel_id=1, source_target_pairs={{0,1},{1,0},{2,3},{3,2},{4,5},{5,4},{6,7},{7,6},{8,9},{9,8},{10,11... | collective-permute-start | bytes 98312 | tf_op jit(solution)/shard_map/ppermute | solution.py:557
  57.2 7.2 %collective-permute-start.5 = (bf16[144,128]{1,0:T(8,128)(2,1)S(1)}, bf16[144,128]{1,0:T(8,128)(2,1)S(1)}, u32[]{:S(2)}, u32[]{:S(2)}) collective-permute-start(bf16[144,128]{1,0:T(8,128)(2,1)S(1)} %pad_maximum_fusion.6), channel_id=1, source_target_pairs={{0,8},{1,9},{2,10},{3,11},{4,12},{5,13},{6,14},{7,15},{8,0},{9,1},... | collective-permute-start | bytes 110600 | tf_op jit(solution)/shard_map/ppermute | solution.py:563
  60.8 10.0 %collective-permute-start.2 = (bf16[256,128]{1,0:T(8,128)(2,1)S(1)}, bf16[256,128]{1,0:T(8,128)(2,1)S(1)}, u32[]{:S(2)}, u32[]{:S(2)}) collective-permute-start(bf16[256,128]{1,0:T(8,128)(2,1)S(1)} %get-tuple-element.31), channel_id=1, source_target_pairs={{1,2},{2,1},{3,4},{4,3},{5,6},{6,5},{7,8},{8,7},{9,10},{10,9},{11,... | collective-permute-start | bytes 196616 | tf_op jit(solution)/shard_map/ppermute | solution.py:542
  61.5 9.4 %collective-permute-start.3 = (bf16[256,128]{1,0:T(8,128)(2,1)S(1)}, bf16[256,128]{1,0:T(8,128)(2,1)S(1)}, u32[]{:S(2)}, u32[]{:S(2)}) collective-permute-start(bf16[256,128]{1,0:T(8,128)(2,1)S(1)} %get-tuple-element.32), channel_id=1, source_target_pairs={{0,1},{1,0},{2,3},{3,2},{4,5},{5,4},{6,7},{7,6},{8,9},{9,8},{10,11... | collective-permute-start | bytes 196616 | tf_op jit(solution)/shard_map/ppermute | solution.py:541
  65.2 4.1 %collective-permute-start.6 = (bf16[160,128]{1,0:T(8,128)(2,1)S(1)}, bf16[160,128]{1,0:T(8,128)(2,1)S(1)}, u32[]{:S(2)}, u32[]{:S(2)}) collective-permute-start(bf16[160,128]{1,0:T(8,128)(2,1)S(1)} %pad_maximum_fusion.5), channel_id=1, source_target_pairs={{0,4},{1,5},{2,6},{3,7},{4,0},{5,1},{6,2},{7,3},{8,12},{9,13},{10,... | collective-permute-start | bytes 122888 | tf_op jit(solution)/shard_map/ppermute | solution.py:563
  69.3 4.2 %collective-permute-start.7 = (bf16[192,128]{1,0:T(8,128)(2,1)S(1)}, bf16[192,128]{1,0:T(8,128)(2,1)S(1)}, u32[]{:S(2)}, u32[]{:S(2)}) collective-permute-start(bf16[192,128]{1,0:T(8,128)(2,1)S(1)} %pad_maximum_fusion.4), channel_id=1, source_target_pairs={{0,2},{1,3},{2,0},{3,1},{4,6},{5,7},{6,4},{7,5},{8,10},{9,11},{10,... | collective-permute-start | bytes 147464 | tf_op jit(solution)/shard_map/ppermute | solution.py:563
  73.5 1.4 %collective-permute-start.8 = (f32[256,128]{1,0:T(8,128)S(1)}, f32[256,128]{1,0:T(8,128)S(1)}, u32[]{:S(2)}, u32[]{:S(2)}) collective-permute-start(f32[256,128]{1,0:T(8,128)S(1)} %pad_maximum_fusion.2), channel_id=1, source_target_pairs={{0,1},{1,0},{2,3},{3,2},{4,5},{5,4},{6,7},{7,6},{8,9},{9,8},{10,11... | collective-permute-start | bytes 393224 | tf_op jit(solution)/shard_map/ppermute | solution.py:572
where the time goes:
time: 77 us; the launch traced here: 76.3 us
  Pallas kernels  40.5 us (53%)
  starting transfers between devices  19.9 us (26%)
  other arithmetic  10.7 us (14%)
  waiting for transfers between devices  3.23 us (4%)
  local copies, waits for them, and re-layouts  1.19 us (2%)
  between operations  0.79 us (1%)
    pallas_call x1, Pallas kernels, per_device(): pl.pallas_call(slope_kernel, out_shape=(jax.ShapeDtypeStruct((edge_count,...  19.3 us
    pallas_call x1, Pallas kernels, per_device(): pl.pallas_call(edge_kernel, out_shape=(jax.ShapeDtypeStruct((fine_count,...  14.8 us
    ppermute x2, starting transfers between devices, pair_exchange(): one = lax.ppermute(jnp.where(even, upward, downward), 'curve', first)  7.31 us
    pallas_call x1, Pallas kernels, per_device(): pl.pallas_call(functools.partial(coarse_kernel, peers), out_shape=jax.Sha...  6.4 us
    ppermute x3, starting transfers between devices, reduced(): lax.ppermute(jnp.concatenate([rounded, coarse], axis=0), 'curve', [(i, i...  5.81 us
    all_to_all x1, starting transfers between devices, per_device(): lax.all_to_all(sent, 'curve', split_axis=0, concat_axis=0, tiled=True)  5.04 us
    ppermute x3, waiting for transfers between devices, reduced(): lax.ppermute(jnp.concatenate([rounded, coarse], axis=0), 'curve', [(i, i...  1.84 us
  transfers between devices with their start and end apart: 10, of which 4 were waited for; matrix products, arithmetic and copies ran while one was open for 9% of the time, Pallas kernels for 34%

commit v1 on v0

--- a/solution.py
+++ b/solution.py
@@ -13,6 +13,7 @@
 SPAN = 256
 EXTRA = 16
 TILE = 512
+GROUP = 4
 SENDERS = 3
 
 F32 = jnp.float32
@@ -190,58 +191,68 @@
             sent_ref[peer, capacity + EXTRA :, :] = share.astype(BF16)
 
 
-def order_edges(recv_ref, off_ref, ordered, stats_vmem, wide, counts, fine_count):
+def order_edges(recv_ref, off_ref, ordered, stats_vmem, positions, fine_count):
     rows = recv_ref.shape[0]
     shift = (fine_count // LANES).bit_length() - 1
     lane = lax.broadcasted_iota(jnp.int32, (LANES, LANES), 1)
     sub = lax.broadcasted_iota(jnp.int32, (LANES, LANES), 0)
-    group = 4
-    counts[...] = jnp.zeros(counts.shape, F32)
-
-    def count(step, carry):
+    level = small(sub)
+    one, zero = jnp.ones((), BF16), jnp.zeros((), BF16)
+
+    def hot(row):
+        return jnp.where(level == small(row), one, zero)
+
+    number = jnp.zeros((LANES, LANES), BF16)
+    for row in range(rows):
+        number += hot(recv_ref[row : row + 1, :] >> shift)
+    ones = jnp.ones((LANES, LANES), BF16)
+    total = dot(number, ones)
+    high = jnp.floor(total * (1.0 / 64.0))
+    low = total - 64.0 * high
+    before = jnp.where(lane < sub, 1.0, 0.0).astype(BF16)
+    start = 64.0 * dot(before, high.astype(BF16)) + dot(before, low.astype(BF16))
+    after = jnp.where(sub < lane, 1.0, 0.0).astype(BF16)
+    prefix = jnp.concatenate([after, ones], axis=1)
+    group = 16
+
+    def place(step, filled):
         for i in range(group):
             row = step * group + i
-            recv = columns(recv_ref[pl.ds(row, 1), :])
-            wide[pl.ds(row * LANES, LANES), :] = recv
-            hot = jnp.where((recv >> shift) == lane, 1.0, 0.0)
-            counts[pl.ds(row, 1), :] = jnp.sum(hot, axis=0, keepdims=True)
-        return carry
-
-    lax.fori_loop(0, rows // group, count, 0)
-    number = counts[...]
-    before_row = jnp.where(lane < sub, 1.0, 0.0).astype(BF16)
-    before_bucket = jnp.where(sub < lane, 1.0, 0.0).astype(BF16)
-    total = jnp.broadcast_to(jnp.sum(number, axis=0, keepdims=True), (8, LANES))
-    high = jnp.floor(total * (1.0 / 64.0))
-    low = total - 64.0 * high
-    start = 64.0 * dot(high.astype(BF16), before_bucket) + dot(low.astype(BF16), before_bucket)
-    counts[...] = dot(before_row, number.astype(BF16)) + start[0:1]
-    lane_place = small(lane)
-    zero = jnp.zeros((), BF16)
-
-    def place(step, moved):
-        left, right = [], []
-        for i in range(group):
-            row = step * group + i
-            recv = wide[pl.ds(row * LANES, LANES), :]
-            off = columns(off_ref[pl.ds(row, 1), :]) + HB
-            bucket = recv >> shift
-            same = (bucket == (recv_ref[pl.ds(row, 1), :] >> shift)) & (lane < sub)
-            mine = jnp.where(bucket == lane, counts[pl.ds(row, 1), :], 0.0)
-            position = jnp.sum(mine + jnp.where(same, 1.0, 0.0), axis=1, keepdims=True)
-            position = jnp.broadcast_to(position, (LANES, LANES)).astype(jnp.int32)
-            here = (position >> 7) == (lane & 63)
-            both = jnp.where(lane < 64, recv & 255, off & 255)
-            rest = ((recv >> 8) << 2) | (off >> 8)
-            first = small(jnp.where(here, both, 0))
-            second = small(jnp.where(here & (lane < 64), rest, 0))
-            left.append(jnp.concatenate([first, second], axis=1))
-            right.append(
-                jnp.where(small(position & 127) == lane_place, jnp.ones((), BF16), zero)
+            bucket = recv_ref[pl.ds(row, 1), :] >> shift
+            found = dot(hot(bucket), prefix)
+            mine = jnp.where(sub == bucket, found[:, 0:LANES] + filled, 0.0)
+            positions[pl.ds(row, 1), :] = jnp.sum(mine, axis=0, keepdims=True).astype(jnp.int32)
+            filled = filled + found[:, LANES:]
+        return filled
+
+    lax.fori_loop(0, rows // group, place, start)
+
+    def move(step, moved):
+        for part in range(0, group, 4):
+            left, right = [], []
+            for i in range(part, part + 4):
+                row = step * group + i
+                position = positions[pl.ds(row, 1), :]
+                recv = recv_ref[pl.ds(row, 1), :]
+                off = off_ref[pl.ds(row, 1), :] + HB
+                rest = ((recv >> 8) << 2) | (off >> 8)
+                here = level[0:64] == small(position >> 7)
+                left.append(
+                    jnp.concatenate(
+                        [
+                            jnp.where(here, small(value), zero)
+                            for value in (recv & 255, off & 255, rest)
+                        ],
+                        axis=0,
+                    )
+                )
+                right.append(hot(position & 127))
+            moved = moved + dot(
+                jnp.concatenate(left, axis=1), jnp.concatenate(right, axis=1), NT
             )
-        return moved + dot(jnp.concatenate(left, axis=0), jnp.concatenate(right, axis=0), TN)
-
-    moved = lax.fori_loop(0, rows // group, place, jnp.zeros((2 * LANES, LANES), F32))
+        return moved
+
+    moved = lax.fori_loop(0, rows // group, move, jnp.zeros((192, LANES), F32))
     moved = moved.astype(jnp.int32)
     rest = moved[LANES : LANES + rows]
     recv = moved[0:rows] + ((rest >> 2) << 8)
@@ -286,14 +297,22 @@
     return recv_base, send_base, fits
 
 
-def either(fits, recv_base, send_base, fine_count, work):
+def each_group(step, stats, fine_count, near, far):
+    tiles = [step * GROUP + i for i in range(GROUP)]
+    places = [tile_bases(stats, tile, fine_count) for tile in tiles]
+    fits = functools.reduce(jnp.logical_and, [place[2] for place in places])
+
     @pl.when(fits)
     def _():
-        work(recv_base, 1, send_base, SENDERS)
+        near(tiles, [place[:2] for place in places])
 
     @pl.when(jnp.logical_not(fits))
     def _():
-        work(0, fine_count // SPAN, 0, fine_count // SPAN + 2)
+        def one(i, carry):
+            far(step * GROUP + i)
+            return carry
+
+        lax.fori_loop(0, GROUP, one, 0)
 
 
 def block_rows(base, block):
@@ -315,21 +334,23 @@
 
 
 def slope_kernel(
+    odd_ref,
     recv_hbm,
     off_hbm,
     fine_hbm,
     weight_hbm,
-    low_hbm,
-    high_hbm,
+    first_hbm,
+    second_hbm,
     slope_hbm,
+    window_out,
     ordered,
     stats_vmem,
     recv_ref,
     off_ref,
     window,
     weight_ref,
-    wide,
-    counts,
+    halos,
+    positions,
     slope_ref,
     stats,
     arrivals,
@@ -338,69 +359,87 @@
 ):
     fine_count = fine_hbm.shape[0]
     copies = fetch(
-        (recv_hbm, off_hbm, fine_hbm, weight_hbm, low_hbm, high_hbm),
+        (recv_hbm, off_hbm, fine_hbm, weight_hbm, first_hbm, second_hbm),
         (
             recv_ref,
             off_ref,
             window.at[pl.ds(HB, fine_count)],
             weight_ref,
-            window.at[pl.ds(0, HB)],
-            window.at[pl.ds(HB + fine_count, HB)],
+            halos.at[0],
+            halos.at[1],
         ),
         arrivals,
     )
     copies[0].wait()
     copies[1].wait()
-    order_edges(recv_ref, off_ref, ordered, stats_vmem, wide, counts, fine_count)
+    order_edges(recv_ref, off_ref, ordered, stats_vmem, positions, fine_count)
     stats_copy = pltpu.make_async_copy(stats_vmem, stats, stats_done)
     stats_copy.start()
     for copy in copies[2:]:
         copy.wait()
+    odd = odd_ref[0]
+    window[0:HB, :] = halos[1 - odd]
+    window[HB + fine_count :, :] = halos[odd]
+    window_copy = pltpu.make_async_copy(window, window_out, leaving.at[leaving.shape[0] - 1])
+    window_copy.start()
     stats_copy.wait()
     count = TILE // LANES
     weight = weight_ref[...]
 
+    def tile_rows(tile):
+        return pl.ds(pl.multiple_of(tile * TILE, TILE), TILE)
+
     def leave(tile):
-        rows = pl.ds(pl.multiple_of(tile * TILE, TILE), TILE)
+        rows = tile_rows(tile)
         return pltpu.make_async_copy(slope_ref.at[rows], slope_hbm.at[rows], leaving.at[tile])
 
-    def step(tile, carry):
-        recv_base, send_base, fits = tile_bases(stats, tile, fine_count)
-
-        def work(recv_base, recv_blocks, send_base, send_blocks):
+    def near(tiles, places):
+        work = []
+        for tile, (recv_base, send_base) in zip(tiles, places):
             recv = index_columns(ordered.at[0], tile * count, count)
             send = index_columns(ordered.at[1], tile * count, count)
-            sender = gather_blocks(send, window, send_base, send_blocks)
-            receiver = gather_blocks(recv + HB, window, recv_base + HB, recv_blocks)
+            sender = gather_blocks(send, window, send_base, SENDERS)
+            receiver = gather_blocks(recv + HB, window, recv_base + HB, 1)
+            work.append((sender, receiver))
+        for tile, (sender, receiver) in zip(tiles, work):
             inputs = jnp.concatenate([sender.astype(BF16), receiver.astype(BF16)], axis=1)
-            slope_ref[pl.ds(pl.multiple_of(tile * TILE, TILE), TILE), :] = silu_slope(
-                dot(inputs, weight)
-            )
-
-        either(fits, recv_base, send_base, fine_count, work)
-        leave(tile).start()
+            slope_ref[tile_rows(tile), :] = silu_slope(dot(inputs, weight))
+
+    def far(tile):
+        recv = index_columns(ordered.at[0], tile * count, count)
+        send = index_columns(ordered.at[1], tile * count, count)
+        sender = gather_blocks(send, window, 0, fine_count // SPAN + 2)
+        receiver = gather_blocks(recv + HB, window, HB, fine_count // SPAN)
+        inputs = jnp.concatenate([sender.astype(BF16), receiver.astype(BF16)], axis=1)
+        slope_ref[tile_rows(tile), :] = silu_slope(dot(inputs, weight))
+
+    def step(index, carry):
+        each_group(index, stats, fine_count, near, far)
+        for i in range(GROUP):
+            leave(index * GROUP + i).start()
         return carry
 
     tiles = slope_ref.shape[0] // TILE
-    lax.fori_loop(0, tiles, step, 0)
+    lax.fori_loop(0, tiles // GROUP, step, 0)
+    window_copy.wait()
     for tile in range(tiles):
         leave(tile).wait()
 
 
 def edge_kernel(
+    odd_ref,
     stats,
     arrived_hbm,
     slots_hbm,
     slope_hbm,
     ordered_hbm,
-    low_hbm,
-    fine_hbm,
-    high_hbm,
+    window_hbm,
     weight_hbm,
     summed_ref,
-    to_prev_ref,
-    to_next_ref,
-    term_ref,
+    first_ref,
+    second_ref,
+    keep_ref,
+    gift_ref,
     coarse_ref,
     gain_ref,
     slot_table,
@@ -416,28 +455,10 @@
     weight_ref,
     arrivals,
 ):
-    fine_count = fine_hbm.shape[0]
+    fine_count = summed_ref.shape[0]
     copies = fetch(
-        (
-            arrived_hbm,
-            slots_hbm,
-            ordered_hbm,
-            slope_hbm,
-            fine_hbm,
-            low_hbm,
-            high_hbm,
-            weight_hbm,
-        ),
-        (
-            arrived_ref,
-            slots_ref,
-            ordered,
-            slope_ref,
-            window.at[pl.ds(HB, fine_count)],
-            window.at[pl.ds(0, HB)],
-            window.at[pl.ds(HB + fine_count, HB)],
-            weight_ref,
-        ),
+        (arrived_hbm, slots_hbm, ordered_hbm, slope_hbm, window_hbm, weight_hbm),
+        (arrived_ref, slots_ref, ordered, slope_ref, window, weight_ref),
         arrivals,
     )
     send_sum[...] = jnp.zeros(send_sum.shape, F32)
@@ -479,44 +500,68 @@
     one, zero = jnp.ones((), BF16), jnp.zeros((), BF16)
     sub = small(lax.broadcasted_iota(jnp.int32, (SPAN, LANES), 0))
 
-    def add_rows(total, base, blocks, at, cols, values):
+    def spread_rows(base, blocks, at, tile, cols, values):
         hot = []
         for i in range(count):
-            row = ordered[at, pl.ds(cols[0] * count + i, 1), :] - base
+            row = ordered[at, pl.ds(tile * count + i, 1), :] - base
             hot.append(jnp.where(sub == small(row & (SPAN - 1)), one, zero))
         hot = jnp.concatenate(hot, axis=1)
         if blocks == 1:
-            total[block_rows(base, 0), :] += dot(hot, values)
-            return
-        block = small((cols[1] - base) >> 8)
+            return [dot(hot, values)]
+        block = small((cols - base) >> 8)
+        parts = []
         for start in range(0, blocks, 2):
             some = range(start, min(start + 2, blocks))
             spread = [jnp.where(block == jnp.full((), j, BF16), values, zero) for j in some]
             part = dot(hot, jnp.concatenate(spread, axis=1))
-            for i, j in enumerate(some):
-                total[block_rows(base, j), :] += part[:, i * LANES : (i + 1) * LANES]
-
-    def step(tile, carry):
-        recv_base, send_base, fits = tile_bases(stats, tile, fine_count)
-
-        def work(recv_base, recv_blocks, send_base, send_blocks):
+            parts += [part[:, i * LANES : (i + 1) * LANES] for i in range(len(some))]
+        return parts
+
+    def add_parts(total, base, parts):
+        for j, part in enumerate(parts):
+            total[block_rows(base, j), :] += part
+
+    def edge_values(tile, recv, base, blocks):
+        upstream = gather_blocks(recv, grad_table, base, blocks)
+        slope = slope_ref[pl.ds(pl.multiple_of(tile * TILE, TILE), TILE), :]
+        return (upstream * slope).astype(BF16)
+
+    def near(tiles, places):
+        work = []
+        for tile, (recv_base, send_base) in zip(tiles, places):
             recv = index_columns(ordered.at[0], tile * count, count)
+            values = edge_values(tile, recv, recv_base, 1)
+            work.append((spread_rows(recv_base, 1, 0, tile, recv, values), values))
+        for (recv_base, _), (parts, _) in zip(places, work):
+            add_parts(recv_sum, recv_base, parts)
+        sums = []
+        for tile, (_, send_base), (_, values) in zip(tiles, places, work):
             send = index_columns(ordered.at[1], tile * count, count)
-            upstream = gather_blocks(recv, grad_table, recv_base, recv_blocks)
-            slope = slope_ref[pl.ds(pl.multiple_of(tile * TILE, TILE), TILE), :]
-            values = (upstream * slope).astype(BF16)
-            add_rows(recv_sum, recv_base, recv_blocks, 0, (tile, recv), values)
-            add_rows(send_sum, send_base, send_blocks, 1, (tile, send), values)
-
-        either(fits, recv_base, send_base, fine_count, work)
+            sums.append(spread_rows(send_base, SENDERS, 1, tile, send, values))
+        for (_, send_base), parts in zip(places, sums):
+            add_parts(send_sum, send_base, parts)
+
+    def far(tile):
+        recv = index_columns(ordered.at[0], tile * count, count)
+        send = index_columns(ordered.at[1], tile * count, count)
+        blocks = fine_count // SPAN
+        values = edge_values(tile, recv, 0, blocks)
+        add_parts(recv_sum, 0, spread_rows(0, blocks, 0, tile, recv, values))
+        add_parts(send_sum, 0, spread_rows(0, blocks + 2, 1, tile, send, values))
+
+    def step(index, carry):
+        each_group(index, stats, fine_count, near, far)
         return carry
 
-    lax.fori_loop(0, slope_ref.shape[0] // TILE, step, 0)
+    lax.fori_loop(0, slope_ref.shape[0] // TILE // GROUP, step, 0)
 
     weight_send = weight_ref[0:LANES, :]
     weight_recv = weight_ref[LANES:, :]
-    to_prev_ref[...] = back(send_sum[0:HB, :], weight_send).astype(BF16)
-    to_next_ref[...] = back(send_sum[HB + fine_count :, :], weight_send).astype(BF16)
+    odd = odd_ref[0]
+    to_prev = back(send_sum[0:HB, :], weight_send)
+    to_next = back(send_sum[HB + fine_count :, :], weight_send)
+    first_ref[...] = jnp.where(odd == 0, to_next, to_prev).astype(BF16)
+    second_ref[...] = jnp.where(odd == 0, to_prev, to_next).astype(BF16)
     term_send = jnp.zeros((LANES, LANES), F32)
     term_recv = jnp.zeros((LANES, LANES), F32)
     for first in range(0, fine_count + 2 * HB, SPAN):
@@ -531,16 +576,14 @@
             + back(send_sum[moved, :], weight_send)
             + back(recv_sum[at, :], weight_recv)
         )
-    term_ref[0:LANES, :] = term_send
-    term_ref[LANES:, :] = term_recv
-
-
-def pair_exchange(upward, downward, even, peers):
-    first = [(i, i ^ 1) for i in range(peers)]
-    second = [(i, ((i + 1) ^ 1) - 1) for i in range(1, peers - 1)]
-    one = lax.ppermute(jnp.where(even, upward, downward), "curve", first)
-    two = lax.ppermute(jnp.where(even, downward, upward), "curve", second)
-    return jnp.where(even, two, one), jnp.where(even, one, two)
+    keep_ref[...] = jnp.where(odd == 0, term_send, term_recv)
+    gift_ref[...] = jnp.where(odd == 0, term_recv, term_send).astype(BF16)
+
+
+def pair_exchange(first, second, peers):
+    pairs = [(i, i ^ 1) for i in range(peers)]
+    between = [(i, ((i + 1) ^ 1) - 1) for i in range(1, peers - 1)]
+    return lax.ppermute(first, "curve", pairs), lax.ppermute(second, "curve", between)
 
 
 def joined(later, own, there):
@@ -549,14 +592,10 @@
     )
 
 
-def reduced(term, coarse, device, peers):
-    half = term.shape[0] // 2
+def reduced(keep, gift, coarse, device, peers):
+    half = keep.shape[0]
     odd = (device & 1) == 1
-    low, high = term[:half], term[half:]
-    gift = jnp.where(odd, low, high).astype(BF16)
-    own = jnp.where(odd, high, low) + lax.ppermute(
-        gift, "curve", [(i, i ^ 1) for i in range(peers)]
-    ).astype(F32)
+    own = keep + lax.ppermute(gift, "curve", [(i, i ^ 1) for i in range(peers)]).astype(F32)
     hops = peers // 2
     while hops > 1:
         rounded = own.astype(BF16)
@@ -591,7 +630,8 @@
 ):
     peers = lax.axis_size("curve")
     device = lax.axis_index("curve")
-    even = (device & 1) == 0
+    odd = (device & 1).astype(jnp.int32)
+    even = odd == 0
     coarse_count = coarse_latent.shape[0]
     fine_count = fine_latent.shape[0]
     edge_count = edge_receivers.shape[0]
@@ -604,7 +644,10 @@
     params = pltpu.CompilerParams(vmem_limit_bytes=64 * 1024 * 1024 - 256 * 1024)
     anywhere = pl.BlockSpec(memory_space=pl.ANY)
 
-    low, high = pair_exchange(fine_latent[fine_count - HB :], fine_latent[:HB], even, peers)
+    head, end = fine_latent[:HB], fine_latent[fine_count - HB :]
+    halos = pair_exchange(jnp.where(even, end, head), jnp.where(even, head, end), peers)
+    parity = odd.reshape(1)
+    scalar = pl.BlockSpec(memory_space=pltpu.SMEM)
 
     sent = pl.pallas_call(
         functools.partial(coarse_kernel, peers),
@@ -637,15 +680,17 @@
     )
     arrived = lax.all_to_all(sent, "curve", split_axis=0, concat_axis=0, tiled=True)
 
-    slope, ordered, stats = pl.pallas_call(
+    slope, window, ordered, stats = pl.pallas_call(
         slope_kernel,
         out_shape=(
             jax.ShapeDtypeStruct((edge_count, LANES), F32),
+            jax.ShapeDtypeStruct((window_count, LANES), BF16),
             jax.ShapeDtypeStruct((2, edge_rows, LANES), jnp.int32),
             jax.ShapeDtypeStruct((edge_rows, LANES), jnp.int32),
         ),
-        in_specs=[anywhere] * 6,
+        in_specs=[scalar] + [anywhere] * 6,
         out_specs=(
+            anywhere,
             anywhere,
             pl.BlockSpec(memory_space=pltpu.VMEM),
             pl.BlockSpec(memory_space=pltpu.VMEM),
@@ -655,13 +700,13 @@
             pltpu.VMEM((edge_rows, LANES), jnp.int32),
             pltpu.VMEM((window_count, LANES), BF16),
             pltpu.VMEM((2 * LANES, LANES), BF16),
-            pltpu.VMEM((edge_count, LANES), jnp.int32),
-            pltpu.VMEM((LANES, LANES), F32),
+            pltpu.VMEM((2, HB, LANES), BF16),
+            pltpu.VMEM((edge_rows, LANES), jnp.int32),
             pltpu.VMEM((edge_count, LANES), F32),
             pltpu.SMEM((edge_rows, LANES), jnp.int32),
             pltpu.SemaphoreType.DMA((6,)),
             pltpu.SemaphoreType.DMA,
-            pltpu.SemaphoreType.DMA((edge_count // TILE,)),
+            pltpu.SemaphoreType.DMA((edge_count // TILE + 1,)),
         ],
         compiler_params=params,
         cost_estimate=pl.CostEstimate(
@@ -669,25 +714,26 @@
         ),
         name="edge_slope",
     )(
+        parity,
         edge_receivers.reshape(-1, LANES),
         edge_offsets.reshape(-1, LANES),
         fine_latent,
         edge_weight,
-        low,
-        high,
-    )
-
-    summed, to_prev, to_next, term_edge, coarse_share, term_gain = pl.pallas_call(
+        *halos,
+    )
+
+    summed, first, second, keep, gift, coarse_share, term_gain = pl.pallas_call(
         edge_kernel,
         out_shape=(
             jax.ShapeDtypeStruct((fine_count, LANES), F32),
             jax.ShapeDtypeStruct((HB, LANES), BF16),
             jax.ShapeDtypeStruct((HB, LANES), BF16),
-            jax.ShapeDtypeStruct((2 * LANES, LANES), F32),
+            jax.ShapeDtypeStruct((LANES, LANES), F32),
+            jax.ShapeDtypeStruct((LANES, LANES), BF16),
             jax.ShapeDtypeStruct((share, LANES), BF16),
             jax.ShapeDtypeStruct((1, LANES), F32),
         ),
-        in_specs=[pl.BlockSpec(memory_space=pltpu.SMEM)] + [anywhere] * 8,
+        in_specs=[scalar] * 2 + [anywhere] * 6,
         scratch_shapes=[
             pltpu.VMEM((SPAN, peers * capacity), BF16),
             pltpu.VMEM((fine_count, LANES), BF16),
@@ -700,7 +746,7 @@
             pltpu.VMEM((2, edge_rows, LANES), jnp.int32),
             pltpu.VMEM((window_count, LANES), BF16),
             pltpu.VMEM((2 * LANES, LANES), BF16),
-            pltpu.SemaphoreType.DMA((8,)),
+            pltpu.SemaphoreType.DMA((6,)),
         ],
         compiler_params=params,
         cost_estimate=pl.CostEstimate(
@@ -708,18 +754,18 @@
         ),
         name="edge_back",
     )(
+        parity,
         stats,
         arrived,
         pair_slots.reshape(-1, LANES),
         slope,
         ordered,
-        low,
-        fine_latent,
-        high,
+        window,
         edge_weight,
     )
-    edge_terms, coarse_terms = reduced(term_edge, coarse_share[:chunk], device, peers)
-    from_prev, from_next = pair_exchange(to_next, to_prev, even, peers)
+    edge_terms, coarse_terms = reduced(keep, gift, coarse_share[:chunk], device, peers)
+    one, two = pair_exchange(first, second, peers)
+    from_next, from_prev = jnp.where(even, one, two), jnp.where(even, two, one)
     coarse_scale = 1.0 / math.sqrt(coarse_count * peers)
     edge_scale = 1.0 / math.sqrt(edge_count * peers)
     grad_fine = jnp.concatenate(

time: 77 us -> 67.1 us (0.87)
  Pallas kernels: 40.5 us -> 28.8 us
  waiting for transfers between devices: 3.23 us -> 10.3 us
  other arithmetic: 10.7 us -> 7.61 us
  starting transfers between devices: 19.9 us -> 17.1 us
    pallas_call x1, Pallas kernels: 19.3 us -> 10.8 us  [per_device(): pl.pallas_call(slope_kernel, out_shape=(jax.ShapeDtypeStruct((edge_count,...]
    ppermute x4, starting transfers between devices: 8.63 us -> 2.52 us  [the longest x2 1.93 us: pair_exchange(): lax.ppermute(second, 'curve', between)]
    all_to_all x1, waiting for transfers between devices: 0.01 us -> 5.21 us  [per_device(): lax.all_to_all(sent, 'curve', split_axis=0, concat_axis=0, tiled=True)]
    all_to_all x1, starting transfers between devices: 5.04 us -> 8.25 us  [per_device(): lax.all_to_all(sent, 'curve', split_axis=0, concat_axis=0, tiled=True)]
    pallas_call x1, Pallas kernels: 14.8 us -> 11.7 us  [per_device(): pl.pallas_call(edge_kernel, out_shape=(jax.ShapeDtypeStruct((fine_count,...]
    select_n x3 -> x1, other arithmetic: 3.06 us -> 0.89 us  [per_device(): jnp.where(even, head, end)]
    ppermute x3, waiting for transfers between devices: 1.84 us -> 3.07 us  [reduced(): lax.ppermute(jnp.concatenate([rounded, coarse], axis=0), 'curve', [(i, i...]
    convert_element_type x1 -> x0, other arithmetic: 0.88 us -> none  [reduced(): gift = jnp.where(odd, low, high).astype(BF16)]
  transfers between devices with their start and end apart: 10 -> 10, of which waited for: 4 -> 6; matrix products, arithmetic and copies ran while one was open for 9% -> 8% of each run, Pallas kernels for 34% -> 26%
where the time goes in v1:
time: 67.1 us; the launch traced here: 66.5 us
  Pallas kernels  28.8 us (43%)
  starting transfers between devices  17.1 us (25%)
  waiting for transfers between devices  10.3 us (15%)
  other arithmetic  7.61 us (11%)
  local copies, waits for them, and re-layouts  1.8 us (3%)
  between operations  0.81 us (1%)
    pallas_call x1, Pallas kernels, per_device(): pl.pallas_call(edge_kernel, out_shape=(jax.ShapeDtypeStruct((fine_count,...  11.7 us
    pallas_call x1, Pallas kernels, per_device(): pl.pallas_call(slope_kernel, out_shape=(jax.ShapeDtypeStruct((edge_count,...  10.8 us
    all_to_all x1, starting transfers between devices, per_device(): lax.all_to_all(sent, 'curve', split_axis=0, concat_axis=0, tiled=True)  8.25 us
    pallas_call x1, Pallas kernels, per_device(): pl.pallas_call(functools.partial(coarse_kernel, peers), out_shape=jax.Sha...  6.4 us
    ppermute x3, starting transfers between devices, reduced(): lax.ppermute(jnp.concatenate([rounded, coarse], axis=0), 'curve', [(i, i...  6.12 us
    all_to_all x1, waiting for transfers between devices, per_device(): lax.all_to_all(sent, 'curve', split_axis=0, concat_axis=0, tiled=True)  5.21 us
    ppermute x3, waiting for transfers between devices, reduced(): lax.ppermute(jnp.concatenate([rounded, coarse], axis=0), 'curve', [(i, i...  3.07 us
    ppermute x2, starting transfers between devices, pair_exchange(): lax.ppermute(second, 'curve', between)  1.93 us
  transfers between devices with their start and end apart: 10, of which 6 were waited for; matrix products, arithmetic and copies ran while one was open for 8% of the time, Pallas kernels for 26%

profile of v1, /device:TPU:0, one launch (start us, length us, event | category | flops | bytes accessed | tf_op | source)
XLA Modules:
  0.0 66.5 jit_solution(8327955026602269523)
XLA Ops:
  0.6 0.9 %broadcast_select_fusion = (bf16[256,128]{1,0:T(8,128)(2,1)S(1)}, bf16[256,128]{1,0:T(8,128)(2,1)S(1)}) fusion(pred[]{:T(512)S(6)} %eq.6, bf16[2048,128]{1,0:T(8,128)(2,1)} %fine_hbm.1), kind=kLoop, calls=%fused_computation.16 | loop fusion | flops 65536 | bytes 262145 | tf_op jit(solution)/shard_map/jit(_where)/select_n | solution.py:648
  2.0 1.3 %collective-permute-start.1 = (bf16[256,128]{1,0:T(8,128)(2,1)S(1)}, bf16[256,128]{1,0:T(8,128)(2,1)}, u32[]{:S(2)}, u32[]{:S(2)}) collective-permute-start(bf16[256,128]{1,0:T(8,128)(2,1)S(1)} %get-tuple-element.29), channel_id=1, source_target_pairs={{1,2},{2,1},{3,4},{4,3},{5,6},{6,5},{7,8},{8,7},{9,10},{10,9},{11,... | collective-permute-start | bytes 196616 | tf_op jit(solution)/shard_map/ppermute | solution.py:586
  3.3 6.4 %coarse_block.1 = bf16[16,160,128]{2,1,0:T(8,128)(2,1)} custom-call(bf16[1024,128]{1,0:T(8,128)(2,1)} %latent_ref.1, bf16[1024,128]{1,0:T(8,128)(2,1)} %grad_ref.1, bf16[2,1024]{1,0:T(2,128)(2,1)} %weights_ref.1, s32[16,128]{1,0:T(8,128)} %bitcast.10, bf16[128,128]{1,0:T(8,128)(2,1)} %w_in_ref.1, bf16[128,128]{1,0:T(8,128)(2,1)} %w_out_ref.1, f32[1,128]{1,0:T(1,128)} %bitcast.12), custom_call_target="tpu_custom_call" | custom-call | flops 2000000000 | bytes 2000000 | tf_op jit(solution)/shard_map/coarse_block/pallas_call | solution.py:652
  9.7 8.2 %all-to-all-start = ((bf16[16,160,128]{2,1,0:T(8,128)(2,1)}), bf16[16,160,128]{2,1,0:T(8,128)(2,1)}, u32[]{:S(2)}, u32[]{:S(2)}) async-start(bf16[16,160,128]{2,1,0:T(8,128)(2,1)} %coarse_block.1), calls=%async_computation | async-start | bytes 1310720 | tf_op jit(solution)/shard_map/all_to_all | solution.py:681
  18.0 0.6 copy-done
  18.6 10.8 %edge_slope.1 = (f32[6144,128]{1,0:T(8,128)}, bf16[2560,128]{1,0:T(8,128)(2,1)}, s32[2,48,128]{2,1,0:T(8,128)}, s32[48,128]{1,0:T(8,128)}) custom-call(s32[1]{0:T(128)} %bitcast.odd_ref, s32[48,128]{1,0:T(8,128)} %bitcast.8, s32[48,128]{1,0:T(8,128)} %bitcast.9, bf16[2048,128]{1,0:T(8,128)(2,1)} %fine_hbm.1, bf16[256,128]{1,0:T(8,128)(2,1)} %weight_hbm.3, ...), custom_call_target="tpu_custom_call" | custom-call | flops 16000000000 | bytes 5000000 | tf_op jit(solution)/shard_map/edge_slope/pallas_call | solution.py:683
  29.4 5.2 %all-to-all-done.arrived_hbm = bf16[16,160,128]{2,1,0:T(8,128)(2,1)} async-done(((bf16[16,160,128]{2,1,0:T(8,128)(2,1)}), bf16[16,160,128]{2,1,0:T(8,128)(2,1)}, u32[]{:S(2)}, u32[]{:S(2)}) %all-to-all-start) | async-done | bytes 655392 | tf_op jit(solution)/shard_map/all_to_all | solution.py:681
  34.6 11.7 %edge_back.1 = (f32[2048,128]{1,0:T(8,128)}, bf16[256,128]{1,0:T(8,128)(2,1)}, bf16[256,128]{1,0:T(8,128)(2,1)}, f32[128,128]{1,0:T(8,128)}, bf16[128,128]{1,0:T...) custom-call(s32[1]{0:T(128)} %bitcast.odd_ref, s32[48,128]{1,0:T(8,128)} %get-tuple-element.16.stats, ...), custom_call_target="tpu_custom_call" | custom-call | flops 24000000000 | bytes 8000000 | tf_op jit(solution)/shard_map/edge_back/pallas_call | solution.py:725
  46.5 1.3 %collective-permute-done.4 = bf16[128,128]{1,0:T(8,128)(2,1)S(1)} collective-permute-done((bf16[128,128]{1,0:T(8,128)(2,1)}, bf16[128,128]{1,0:T(8,128)(2,1)S(1)}, u32[]{:S(2)}, u32[]{:S(2)}) %collective-permute-start.4) | collective-permute-done | bytes 32800 | tf_op jit(solution)/shard_map/ppermute | solution.py:598
  47.8 0.8 %add_convert_fusion.4 = bf16[128,128]{1,0:T(8,128)(2,1)S(1)} fusion(f32[128,128]{1,0:T(8,128)} %get-tuple-element.23, bf16[128,128]{1,0:T(8,128)(2,1)S(1)} %collective-permute-done.4), kind=kLoop, calls=%fused_computation.15 | loop fusion | flops 49152 | bytes 131072 | tf_op jit(solution)/shard_map/convert_element_type | solution.py:601
  48.6 0.7 %pad_maximum_fusion.6 = bf16[144,128]{1,0:T(8,128)(2,1)S(1)} fusion(bf16[16,128]{1,0:T(8,128)(2,1)} %get-tuple-element.25, bf16[128,128]{1,0:T(8,128)(2,1)S(1)} %add_convert_fusion.4), kind=kLoop, calls=%fused_computation.20 | loop fusion | flops 73728 | bytes 73728 | tf_op jit(solution)/shard_map/concatenate | solution.py:603
  49.3 2.9 %collective-permute-start.5 = (bf16[144,128]{1,0:T(8,128)(2,1)S(1)}, bf16[144,128]{1,0:T(8,128)(2,1)S(1)}, u32[]{:S(2)}, u32[]{:S(2)}) collective-permute-start(bf16[144,128]{1,0:T(8,128)(2,1)S(1)} %pad_maximum_fusion.6), channel_id=1, source_target_pairs={{0,8},{1,9},{2,10},{3,11},{4,12},{5,13},{6,14},{7,15},{8,0},{9,1},... | collective-permute-start | bytes 110600 | tf_op jit(solution)/shard_map/ppermute | solution.py:602
  52.3 0.7 collective-permute-start.2
  52.9 1.3 %collective-permute-done.5 = bf16[144,128]{1,0:T(8,128)(2,1)S(1)} collective-permute-done((bf16[144,128]{1,0:T(8,128)(2,1)S(1)}, bf16[144,128]{1,0:T(8,128)(2,1)S(1)}, u32[]{:S(2)}, u32[]{:S(2)}) %collective-permute-start.5) | collective-permute-done | bytes 36896 | tf_op jit(solution)/shard_map/ppermute | solution.py:602
  54.2 0.8 %maximum_select_fusion.2 = bf16[32,128]{1,0:T(8,128)(2,1)S(1)} fusion(bf16[16,128]{1,0:T(8,128)(2,1)} %get-tuple-element.25, bf16[16,128]{1,0:T(8,128)(2,1)S(1)} %slice.63, pred[]{:T(512)S(6)} %ne.9), kind=kLoop, calls=%fused_computation.24 | loop fusion | flops 36864 | bytes 16385 | tf_op jit(solution)/shard_map/jit(_where)/select_n | solution.py:590
  55.0 2.0 %collective-permute-start.6 = (bf16[160,128]{1,0:T(8,128)(2,1)S(1)}, bf16[160,128]{1,0:T(8,128)(2,1)S(1)}, u32[]{:S(2)}, u32[]{:S(2)}) collective-permute-start(bf16[160,128]{1,0:T(8,128)(2,1)S(1)} %pad_maximum_fusion.5), channel_id=1, source_target_pairs={{0,4},{1,5},{2,6},{3,7},{4,0},{5,1},{6,2},{7,3},{8,12},{9,13},{10,... | collective-permute-start | bytes 122888 | tf_op jit(solution)/shard_map/ppermute | solution.py:602
  57.0 1.2 %multiply_bitcast_fusion = f32[128]{0:T(128)} fusion(f32[1,128]{1,0:T(1,128)} %get-tuple-element.26), kind=kLoop, calls=%fused_computation.25 | loop fusion | flops 128 | bytes 1024 | tf_op jit(solution)/shard_map/mul | solution.py:784
  58.2 1.2 %slice.84 = bf16[1536,128]{1,0:T(8,128)(2,1)S(1)} slice(f32[2048,128]{1,0:T(8,128)} %get-tuple-element.20), slice={[256:1792], [0:128]} | slice | bytes 786432 | tf_op jit(solution)/shard_map/slice | solution.py:774
  59.5 1.2 %collective-permute-start.7 = (bf16[192,128]{1,0:T(8,128)(2,1)S(1)}, bf16[192,128]{1,0:T(8,128)(2,1)S(1)}, u32[]{:S(2)}, u32[]{:S(2)}) collective-permute-start(bf16[192,128]{1,0:T(8,128)(2,1)S(1)} %pad_maximum_fusion.4), channel_id=1, source_target_pairs={{0,2},{1,3},{2,0},{3,1},{4,6},{5,7},{6,4},{7,5},{8,10},{9,11},{10,... | collective-permute-start | bytes 147464 | tf_op jit(solution)/shard_map/ppermute | solution.py:602
  60.9 1.0 %add_convert_fusion.1 = (bf16[256,128]{1,0:T(8,128)(2,1)S(1)}, bf16[256,128]{1,0:T(8,128)(2,1)S(1)}) fusion(f32[2048,128]{1,0:T(8,128)} %get-tuple-element.20, bf16[256,128]{1,0:T(8,128)(2,1)S(1)} %collective-permute-done.2, bf16[256,128]{1,0:T(8,128)(2,1)S(1)} %collective-permute-done.3, pred[]{:T(512)S(6)} %eq.6), kind=kLoop, calls=%fused_computation.9 | loop fusion | flops 262144 | bytes 524289 | tf_op jit(solution)/shard_map/convert
  61.9 1.8 %collective-permute-done.7 = bf16[192,128]{1,0:T(8,128)(2,1)S(1)} collective-permute-done((bf16[192,128]{1,0:T(8,128)(2,1)S(1)}, bf16[192,128]{1,0:T(8,128)(2,1)S(1)}, u32[]{:S(2)}, u32[]{:S(2)}) %collective-permute-start.7) | collective-permute-done | bytes 49184 | tf_op jit(solution)/shard_map/ppermute | solution.py:602
  63.8 0.8 %pad_maximum_fusion = bf16[2048,128]{1,0:T(8,128)(2,1)} fusion(bf16[256,128]{1,0:T(8,128)(2,1)S(1)} %get-tuple-element.28, bf16[1536,128]{1,0:T(8,128)(2,1)S(1)} %slice.84, bf16[256,128]{1,0:T(8,128)(2,1)S(1)} %get-tuple-element.27), kind=kLoop, calls=%fused_computation.1 | loop fusion | flops 1572864 | bytes 1048576 | tf_op jit(solution)/shard_map/concatenate | solution.py:771
  65.2 0.7 %fusion.1 = (f32[256,128]{1,0:T(8,128)}, f32[256,128]{1,0:T(8,128)S(1)}) fusion(f32[128,128]{1,0:T(8,128)S(1)} %convert_add_fusion, f32[128,128]{1,0:T(8,128)S(1)} %get-tuple-element.34, pred[]{:T(512)S(6)} %eq.7, f32[128,128]{1,0:T(8,128)S(1)} %get-tuple-element.33, f32[128,128]{1,0:T(8,128)S(1)} %fusion.3), kind=kLoop, calls=%fused_computation.6 | loop fusion | flops 229376 | bytes 524289 | tf_op jit(solution)/shard_map/mul | solution.py:781
  65.9 0.7 slice_multiply_fusion
  (23 shorter events, 1.6 us)
Async XLA Ops:
  1.5 16.5 %collective-permute-start = (bf16[256,128]{1,0:T(8,128)(2,1)S(1)}, bf16[256,128]{1,0:T(8,128)(2,1)S(1)}, u32[]{:S(2)}, u32[]{:S(2)}) collective-permute-start(bf16[256,128]{1,0:T(8,128)(2,1)S(1)} %get-tuple-element.30), channel_id=1, source_target_pairs={{0,1},{1,0},{2,3},{3,2},{4,5},{5,4},{6,7},{7,6},{8,9},{9,8},{10,11... | collective-permute-start | bytes 196616 | tf_op jit(solution)/shard_map/ppermute | solution.py:586
  2.0 16.0 %collective-permute-start.1 = (bf16[256,128]{1,0:T(8,128)(2,1)S(1)}, bf16[256,128]{1,0:T(8,128)(2,1)}, u32[]{:S(2)}, u32[]{:S(2)}) collective-permute-start(bf16[256,128]{1,0:T(8,128)(2,1)S(1)} %get-tuple-element.29), channel_id=1, source_target_pairs={{1,2},{2,1},{3,4},{4,3},{5,6},{6,5},{7,8},{8,7},{9,10},{10,9},{11,... | collective-permute-start | bytes 196616 | tf_op jit(solution)/shard_map/ppermute | solution.py:586
  9.7 24.9 %all-to-all-start = ((bf16[16,160,128]{2,1,0:T(8,128)(2,1)}), bf16[16,160,128]{2,1,0:T(8,128)(2,1)}, u32[]{:S(2)}, u32[]{:S(2)}) async-start(bf16[16,160,128]{2,1,0:T(8,128)(2,1)} %coarse_block.1), calls=%async_computation | async-start | bytes 1310720 | tf_op jit(solution)/shard_map/all_to_all | solution.py:681
  18.0 0.6 copy-start
  46.3 1.5 %collective-permute-start.4 = (bf16[128,128]{1,0:T(8,128)(2,1)}, bf16[128,128]{1,0:T(8,128)(2,1)S(1)}, u32[]{:S(2)}, u32[]{:S(2)}) collective-permute-start(bf16[128,128]{1,0:T(8,128)(2,1)} %get-tuple-element.24), channel_id=1, source_target_pairs={{0,1},{1,0},{2,3},{3,2},{4,5},{5,4},{6,7},{7,6},{8,9},{9,8},{10,11... | collective-permute-start | bytes 98312 | tf_op jit(solution)/shard_map/ppermute | solution.py:598
  49.3 4.9 %collective-permute-start.5 = (bf16[144,128]{1,0:T(8,128)(2,1)S(1)}, bf16[144,128]{1,0:T(8,128)(2,1)S(1)}, u32[]{:S(2)}, u32[]{:S(2)}) collective-permute-start(bf16[144,128]{1,0:T(8,128)(2,1)S(1)} %pad_maximum_fusion.6), channel_id=1, source_target_pairs={{0,8},{1,9},{2,10},{3,11},{4,12},{5,13},{6,14},{7,15},{8,0},{9,1},... | collective-permute-start | bytes 110600 | tf_op jit(solution)/shard_map/ppermute | solution.py:602
  52.3 8.4 %collective-permute-start.2 = (bf16[256,128]{1,0:T(8,128)(2,1)}, bf16[256,128]{1,0:T(8,128)(2,1)S(1)}, u32[]{:S(2)}, u32[]{:S(2)}) collective-permute-start(bf16[256,128]{1,0:T(8,128)(2,1)} %get-tuple-element.21), channel_id=1, source_target_pairs={{1,2},{2,1},{3,4},{4,3},{5,6},{6,5},{7,8},{8,7},{9,10},{10,9},{11,... | collective-permute-start | bytes 196616 | tf_op jit(solution)/shard_map/ppermute | solution.py:586
  55.0 4.4 %collective-permute-start.6 = (bf16[160,128]{1,0:T(8,128)(2,1)S(1)}, bf16[160,128]{1,0:T(8,128)(2,1)S(1)}, u32[]{:S(2)}, u32[]{:S(2)}) collective-permute-start(bf16[160,128]{1,0:T(8,128)(2,1)S(1)} %pad_maximum_fusion.5), channel_id=1, source_target_pairs={{0,4},{1,5},{2,6},{3,7},{4,0},{5,1},{6,2},{7,3},{8,12},{9,13},{10,... | collective-permute-start | bytes 122888 | tf_op jit(solution)/shard_map/ppermute | solution.py:602
  59.4 1.5 %collective-permute-start.3 = (bf16[256,128]{1,0:T(8,128)(2,1)}, bf16[256,128]{1,0:T(8,128)(2,1)S(1)}, u32[]{:S(2)}, u32[]{:S(2)}) collective-permute-start(bf16[256,128]{1,0:T(8,128)(2,1)} %get-tuple-element.22), channel_id=1, source_target_pairs={{0,1},{1,0},{2,3},{3,2},{4,5},{5,4},{6,7},{7,6},{8,9},{9,8},{10,11... | collective-permute-start | bytes 196616 | tf_op jit(solution)/shard_map/ppermute | solution.py:586
  59.5 4.2 %collective-permute-start.7 = (bf16[192,128]{1,0:T(8,128)(2,1)S(1)}, bf16[192,128]{1,0:T(8,128)(2,1)S(1)}, u32[]{:S(2)}, u32[]{:S(2)}) collective-permute-start(bf16[192,128]{1,0:T(8,128)(2,1)S(1)} %pad_maximum_fusion.4), channel_id=1, source_target_pairs={{0,2},{1,3},{2,0},{3,1},{4,6},{5,7},{6,4},{7,5},{8,10},{9,11},{10,... | collective-permute-start | bytes 147464 | tf_op jit(solution)/shard_map/ppermute | solution.py:602
  63.7 1.4 %collective-permute-start.8 = (f32[256,128]{1,0:T(8,128)S(1)}, f32[256,128]{1,0:T(8,128)S(1)}, u32[]{:S(2)}, u32[]{:S(2)}) collective-permute-start(f32[256,128]{1,0:T(8,128)S(1)} %pad_maximum_fusion.2), channel_id=1, source_target_pairs={{0,1},{1,0},{2,3},{3,2},{4,5},{5,4},{6,7},{7,6},{8,9},{9,8},{10,11... | collective-permute-start | bytes 393224 | tf_op jit(solution)/shard_map/ppermute | solution.py:611

commit v2 on v1

--- a/solution.py
+++ b/solution.py
@@ -53,12 +53,10 @@
     )
 
 
-def gather_rows(cols, table, width):
-    hot = place_hot(cols)
-    block = cols // SPAN
+def gather_rows(hot, block, table, width):
     total = table.shape[1]
     step = max(width, 2 * LANES)
-    found = [jnp.zeros(cols.shape, F32) for _ in range(width // LANES)]
+    found = [jnp.zeros(block.shape, F32) for _ in range(width // LANES)]
     for start in range(0, total, step):
         part = dot(hot, table[:, start : start + step])
         for inner in range(0, step, width):
@@ -67,6 +65,37 @@
                 at = inner + i * LANES
                 found[i] = jnp.where(here, part[:, at : at + LANES], found[i])
     return found
+
+
+def spread_rows(hot, block, blocks, values):
+    if blocks == 1:
+        return [dot(hot, values)]
+    parts = []
+    zero = jnp.zeros((), BF16)
+    for start in range(0, blocks, 2):
+        some = range(start, min(start + 2, blocks))
+        spread = [jnp.where(block == jnp.full((), j, BF16), values, zero) for j in some]
+        part = dot(hot, jnp.concatenate(spread, axis=1))
+        parts += [part[:, i * LANES : (i + 1) * LANES] for i in range(len(some))]
+    return parts
+
+
+def add_parts(total, base, parts):
+    for j, part in enumerate(parts):
+        total[block_rows(base, j), :] += part
+
+
+def place_hot_rows(ordered, at, tile, base, level):
+    one, zero = jnp.ones((), BF16), jnp.zeros((), BF16)
+    hot = []
+    for i in range(TILE // LANES):
+        row = ordered[at, pl.ds(tile * (TILE // LANES) + i, 1), :] - base
+        hot.append(jnp.where(level == small(row & (SPAN - 1)), one, zero))
+    return jnp.concatenate(hot, axis=1)
+
+
+def levels():
+    return small(lax.broadcasted_iota(jnp.int32, (SPAN, LANES), 0))
 
 
 def two_parts(values):
@@ -127,36 +156,33 @@
     chunk = SPAN // peers
     capacity = sent_ref.shape[1] - EXTRA - max(EXTRA, chunk)
     w_in, w_out, gain = w_in_ref[...], w_out_ref[...], gain_ref[...]
-    term_in = jnp.zeros((LANES, LANES), F32)
-    term_out = jnp.zeros((LANES, LANES), F32)
-    term_gain = jnp.zeros((1, LANES), F32)
+    latent = latent_ref[...]
+    pre = dot(latent, w_in)
+    sigm = jax.nn.sigmoid(pre)
+    hidden = (pre * sigm).astype(BF16)
+    slope = sigm * (1.0 + pre * (1.0 - sigm))
+    mapped = dot(hidden, w_out)
+    centred = mapped - jnp.mean(mapped, axis=1, keepdims=True)
+    inverse = lax.rsqrt(jnp.mean(centred * centred, axis=1, keepdims=True) + 1e-05)
+    normed = centred * inverse
+    upstream = grad_ref[...].astype(F32)
+    scaled = upstream * gain
+    grad_mapped = (
+        inverse
+        * (
+            scaled
+            - jnp.mean(scaled, axis=1, keepdims=True)
+            - normed * jnp.mean(scaled * normed, axis=1, keepdims=True)
+        )
+    ).astype(BF16)
+    grad_pre = (dot(grad_mapped, w_out, NT) * slope).astype(BF16)
+    grad_in = (upstream + dot(grad_pre, w_in, NT)).astype(BF16)
+    term_gain = jnp.sum(upstream * normed, axis=0, keepdims=True)
+    term_in = dot(latent, grad_pre, TN)
+    term_out = dot(hidden, grad_mapped, TN)
     for block in range(count // SPAN):
-        rows = pl.ds(block * SPAN, SPAN)
-        latent = latent_ref[rows, :]
-        pre = dot(latent, w_in)
-        sigm = jax.nn.sigmoid(pre)
-        hidden = (pre * sigm).astype(BF16)
-        slope = sigm * (1.0 + pre * (1.0 - sigm))
-        mapped = dot(hidden, w_out)
-        centred = mapped - jnp.mean(mapped, axis=1, keepdims=True)
-        inverse = lax.rsqrt(jnp.mean(centred * centred, axis=1, keepdims=True) + 1e-05)
-        normed = centred * inverse
-        upstream = grad_ref[rows, :].astype(F32)
-        scaled = upstream * gain
-        grad_mapped = (
-            inverse
-            * (
-                scaled
-                - jnp.mean(scaled, axis=1, keepdims=True)
-                - normed * jnp.mean(scaled * normed, axis=1, keepdims=True)
-            )
-        ).astype(BF16)
-        grad_pre = (dot(grad_mapped, w_out, NT) * slope).astype(BF16)
-        grad_in = (upstream + dot(grad_pre, w_in, NT)).astype(BF16)
-        term_gain += jnp.sum(upstream * normed, axis=0, keepdims=True)
-        term_in += dot(latent, grad_pre, TN)
-        term_out += dot(hidden, grad_mapped, TN)
-        table_ref[:, block * SPAN : block * SPAN + LANES] = grad_in
+        at = block * SPAN
+        table_ref[:, at : at + LANES] = grad_in[at : at + SPAN]
         for half in range(SPAN // LANES):
             at = block * SPAN + half * LANES
             pair = weights_ref[:, at : at + LANES].astype(F32)
@@ -170,7 +196,7 @@
     per_step = 256 // LANES
     for first in range(0, rows_ref.shape[0], per_step):
         cols = index_columns(rows_ref, first, per_step)
-        sent, weight = gather_rows(cols, table_ref[...], SPAN)
+        sent, weight = gather_rows(place_hot(cols), cols // SPAN, table_ref, SPAN)
         for part in range(per_step * LANES // capacity):
             peer = first * LANES // capacity + part
             rows = slice(part * capacity, (part + 1) * capacity)
@@ -319,10 +345,7 @@
     return pl.ds(pl.multiple_of(base + block * SPAN, 16), SPAN)
 
 
-def gather_blocks(cols, table, base, blocks):
-    local = cols - base
-    hot = place_hot(local)
-    block = local >> 8
+def gather_blocks(hot, block, table, base, blocks):
     found = None
     for start in range(0, blocks, 2):
         some = range(start, min(start + 2, blocks))
@@ -333,36 +356,50 @@
     return found
 
 
+def tile_rows(tile):
+    return pl.ds(pl.multiple_of(tile * TILE, TILE), TILE)
+
+
 def slope_kernel(
-    odd_ref,
     recv_hbm,
     off_hbm,
+    slots_hbm,
     fine_hbm,
     weight_hbm,
     first_hbm,
     second_hbm,
     slope_hbm,
-    window_out,
+    hot_hbm,
+    block_hbm,
+    window_hbm,
+    slope_sum,
     ordered,
     stats_vmem,
+    slot_hot,
+    slot_block,
     recv_ref,
     off_ref,
+    slots_ref,
     window,
     weight_ref,
     halos,
     positions,
     slope_ref,
+    hot_ref,
+    block_ref,
     stats,
     arrivals,
     stats_done,
     leaving,
+    window_left,
 ):
     fine_count = fine_hbm.shape[0]
     copies = fetch(
-        (recv_hbm, off_hbm, fine_hbm, weight_hbm, first_hbm, second_hbm),
+        (recv_hbm, off_hbm, slots_hbm, fine_hbm, weight_hbm, first_hbm, second_hbm),
         (
             recv_ref,
             off_ref,
+            slots_ref,
             window.at[pl.ds(HB, fine_count)],
             weight_ref,
             halos.at[0],
@@ -377,98 +414,155 @@
     stats_copy.start()
     for copy in copies[2:]:
         copy.wait()
-    odd = odd_ref[0]
+    slope_sum[...] = jnp.zeros(slope_sum.shape, F32)
+    slots = index_columns(slots_ref, 0, slots_ref.shape[0])
+    slot_hot[...] = place_hot(slots)
+    slot_block[...] = slots // SPAN
+    odd = lax.axis_index("curve") & 1
     window[0:HB, :] = halos[1 - odd]
     window[HB + fine_count :, :] = halos[odd]
-    window_copy = pltpu.make_async_copy(window, window_out, leaving.at[leaving.shape[0] - 1])
+    window_copy = pltpu.make_async_copy(window, window_hbm, window_left)
     window_copy.start()
     stats_copy.wait()
     count = TILE // LANES
     weight = weight_ref[...]
-
-    def tile_rows(tile):
-        return pl.ds(pl.multiple_of(tile * TILE, TILE), TILE)
+    level = levels()
 
     def leave(tile):
         rows = tile_rows(tile)
-        return pltpu.make_async_copy(slope_ref.at[rows], slope_hbm.at[rows], leaving.at[tile])
+        pairs = ((slope_ref, slope_hbm), (hot_ref, hot_hbm), (block_ref, block_hbm))
+        return [
+            pltpu.make_async_copy(source.at[rows], target.at[rows], leaving.at[i, tile])
+            for i, (source, target) in enumerate(pairs)
+        ]
 
     def near(tiles, places):
         work = []
         for tile, (recv_base, send_base) in zip(tiles, places):
-            recv = index_columns(ordered.at[0], tile * count, count)
-            send = index_columns(ordered.at[1], tile * count, count)
-            sender = gather_blocks(send, window, send_base, SENDERS)
-            receiver = gather_blocks(recv + HB, window, recv_base + HB, 1)
+            recv = index_columns(ordered.at[0], tile * count, count) - recv_base
+            send = index_columns(ordered.at[1], tile * count, count) - send_base
+            block = send >> 8
+            hot = place_hot(recv)
+            hot_ref[tile_rows(tile), :] = hot
+            block_ref[tile_rows(tile), :] = small(block)
+            sender = gather_blocks(place_hot(send), block, window, send_base, SENDERS)
+            receiver = gather_blocks(hot, None, window, recv_base + HB, 1)
             work.append((sender, receiver))
+        slopes = []
         for tile, (sender, receiver) in zip(tiles, work):
             inputs = jnp.concatenate([sender.astype(BF16), receiver.astype(BF16)], axis=1)
-            slope_ref[tile_rows(tile), :] = silu_slope(dot(inputs, weight))
+            slope = silu_slope(dot(inputs, weight))
+            slope_ref[tile_rows(tile), :] = slope
+            slopes.append(jnp.concatenate(two_parts(slope), axis=1))
+        sums = []
+        for tile, (recv_base, _), slope in zip(tiles, places, slopes):
+            hot = place_hot_rows(ordered, 0, tile, recv_base, level)
+            both = dot(hot, slope)
+            sums.append(both[:, 0:LANES] + both[:, LANES:])
+        for (recv_base, _), part in zip(places, sums):
+            add_parts(slope_sum, recv_base, [part])
 
     def far(tile):
         recv = index_columns(ordered.at[0], tile * count, count)
         send = index_columns(ordered.at[1], tile * count, count)
-        sender = gather_blocks(send, window, 0, fine_count // SPAN + 2)
-        receiver = gather_blocks(recv + HB, window, HB, fine_count // SPAN)
+        blocks = fine_count // SPAN
+        sender = gather_blocks(place_hot(send), send >> 8, window, 0, blocks + 2)
+        receiver = gather_blocks(place_hot(recv), recv >> 8, window, HB, blocks)
         inputs = jnp.concatenate([sender.astype(BF16), receiver.astype(BF16)], axis=1)
-        slope_ref[tile_rows(tile), :] = silu_slope(dot(inputs, weight))
+        slope = silu_slope(dot(inputs, weight))
+        slope_ref[tile_rows(tile), :] = slope
+        hot = place_hot_rows(ordered, 0, tile, 0, level)
+        for part in two_parts(slope):
+            add_parts(slope_sum, 0, spread_rows(hot, small(recv >> 8), blocks, part))
+        hot_ref[tile_rows(tile), :] = jnp.zeros((TILE, SPAN), BF16)
+        block_ref[tile_rows(tile), :] = jnp.zeros((TILE, LANES), BF16)
 
     def step(index, carry):
         each_group(index, stats, fine_count, near, far)
         for i in range(GROUP):
-            leave(index * GROUP + i).start()
+            for copy in leave(index * GROUP + i):
+                copy.start()
         return carry
 
     tiles = slope_ref.shape[0] // TILE
     lax.fori_loop(0, tiles // GROUP, step, 0)
     window_copy.wait()
     for tile in range(tiles):
-        leave(tile).wait()
+        for copy in leave(tile):
+            copy.wait()
 
 
 def edge_kernel(
-    odd_ref,
+    coarse_scale,
     stats,
     arrived_hbm,
-    slots_hbm,
+    slot_hot_hbm,
+    slot_block_hbm,
+    hot_hbm,
     slope_hbm,
+    block_hbm,
     ordered_hbm,
     window_hbm,
+    slope_sum_hbm,
     weight_hbm,
-    summed_ref,
+    fine_ref,
+    ends_ref,
     first_ref,
     second_ref,
     keep_ref,
     gift_ref,
-    coarse_ref,
     gain_ref,
     slot_table,
     grad_table,
     grad_rows,
     send_sum,
-    recv_sum,
     arrived_ref,
-    slots_ref,
+    slot_hot,
+    slot_block,
+    hot_ref,
     slope_ref,
+    block_ref,
     ordered,
     window,
+    slope_sum,
     weight_ref,
     arrivals,
 ):
-    fine_count = summed_ref.shape[0]
+    fine_count = fine_ref.shape[0]
     copies = fetch(
-        (arrived_hbm, slots_hbm, ordered_hbm, slope_hbm, window_hbm, weight_hbm),
-        (arrived_ref, slots_ref, ordered, slope_ref, window, weight_ref),
+        (
+            arrived_hbm,
+            slot_hot_hbm,
+            slot_block_hbm,
+            hot_hbm,
+            slope_hbm,
+            block_hbm,
+            ordered_hbm,
+            window_hbm,
+            slope_sum_hbm,
+            weight_hbm,
+        ),
+        (
+            arrived_ref,
+            slot_hot,
+            slot_block,
+            hot_ref,
+            slope_ref,
+            block_ref,
+            ordered,
+            window,
+            slope_sum,
+            weight_ref,
+        ),
         arrivals,
     )
     send_sum[...] = jnp.zeros(send_sum.shape, F32)
-    recv_sum[...] = jnp.zeros(recv_sum.shape, F32)
     peers = arrived_ref.shape[0]
     share = max(EXTRA, SPAN // peers)
     capacity = arrived_ref.shape[1] - EXTRA - share
     per_block = SPAN // capacity
-    copies[0].wait()
-    copies[1].wait()
+    for copy in copies[:3]:
+        copy.wait()
     coarse = jnp.zeros((share, LANES), F32)
     gain = jnp.zeros((1, LANES), F32)
     for peer in range(peers):
@@ -482,72 +576,44 @@
         )
         gain += extra[2:3] + extra[3:4]
         coarse += arrived_ref[peer, capacity + EXTRA :, :].astype(F32)
-    coarse_ref[...] = coarse.astype(BF16)
-    gain_ref[...] = gain
-
-    per_step = SPAN // LANES
-    for first in range(0, slots_ref.shape[0], per_step):
-        cols = index_columns(slots_ref, first, per_step)
-        grad, weight = gather_rows(cols, slot_table, SPAN)
+    keep_ref[LANES:, :] = coarse
+    gain_ref[...] = gain * coarse_scale
+
+    for first in range(0, slot_hot.shape[0], SPAN):
+        at = slice(first, first + SPAN)
+        grad, weight = gather_rows(slot_hot[at, :], slot_block[at, :], slot_table, SPAN)
         for r in range(2):
             rows = (grad * weight[:, r : r + 1]).astype(BF16).astype(F32)
-            grad_rows[pl.ds(2 * first * LANES + r, SPAN, stride=2), :] = rows
+            grad_rows[pl.ds(2 * first + r, SPAN, stride=2), :] = rows
     grad_table[...] = grad_rows[...].astype(BF16)
-    for copy in copies[2:]:
+    for copy in copies[3:]:
         copy.wait()
 
     count = TILE // LANES
-    one, zero = jnp.ones((), BF16), jnp.zeros((), BF16)
-    sub = small(lax.broadcasted_iota(jnp.int32, (SPAN, LANES), 0))
-
-    def spread_rows(base, blocks, at, tile, cols, values):
-        hot = []
-        for i in range(count):
-            row = ordered[at, pl.ds(tile * count + i, 1), :] - base
-            hot.append(jnp.where(sub == small(row & (SPAN - 1)), one, zero))
-        hot = jnp.concatenate(hot, axis=1)
-        if blocks == 1:
-            return [dot(hot, values)]
-        block = small((cols - base) >> 8)
-        parts = []
-        for start in range(0, blocks, 2):
-            some = range(start, min(start + 2, blocks))
-            spread = [jnp.where(block == jnp.full((), j, BF16), values, zero) for j in some]
-            part = dot(hot, jnp.concatenate(spread, axis=1))
-            parts += [part[:, i * LANES : (i + 1) * LANES] for i in range(len(some))]
-        return parts
-
-    def add_parts(total, base, parts):
-        for j, part in enumerate(parts):
-            total[block_rows(base, j), :] += part
-
-    def edge_values(tile, recv, base, blocks):
-        upstream = gather_blocks(recv, grad_table, base, blocks)
-        slope = slope_ref[pl.ds(pl.multiple_of(tile * TILE, TILE), TILE), :]
-        return (upstream * slope).astype(BF16)
+    level = levels()
 
     def near(tiles, places):
         work = []
-        for tile, (recv_base, send_base) in zip(tiles, places):
-            recv = index_columns(ordered.at[0], tile * count, count)
-            values = edge_values(tile, recv, recv_base, 1)
-            work.append((spread_rows(recv_base, 1, 0, tile, recv, values), values))
-        for (recv_base, _), (parts, _) in zip(places, work):
-            add_parts(recv_sum, recv_base, parts)
+        for tile, (recv_base, _) in zip(tiles, places):
+            rows = tile_rows(tile)
+            upstream = gather_blocks(hot_ref[rows, :], None, grad_table, recv_base, 1)
+            work.append((upstream * slope_ref[rows, :]).astype(BF16))
         sums = []
-        for tile, (_, send_base), (_, values) in zip(tiles, places, work):
-            send = index_columns(ordered.at[1], tile * count, count)
-            sums.append(spread_rows(send_base, SENDERS, 1, tile, send, values))
+        for tile, (_, send_base), values in zip(tiles, places, work):
+            hot = place_hot_rows(ordered, 1, tile, send_base, level)
+            sums.append(spread_rows(hot, block_ref[tile_rows(tile), :], SENDERS, values))
         for (_, send_base), parts in zip(places, sums):
             add_parts(send_sum, send_base, parts)
 
     def far(tile):
+        rows = tile_rows(tile)
         recv = index_columns(ordered.at[0], tile * count, count)
         send = index_columns(ordered.at[1], tile * count, count)
         blocks = fine_count // SPAN
-        values = edge_values(tile, recv, 0, blocks)
-        add_parts(recv_sum, 0, spread_rows(0, blocks, 0, tile, recv, values))
-        add_parts(send_sum, 0, spread_rows(0, blocks + 2, 1, tile, send, values))
+        upstream = gather_blocks(place_hot(recv), recv >> 8, grad_table, 0, blocks)
+        values = (upstream * slope_ref[rows, :]).astype(BF16)
+        hot = place_hot_rows(ordered, 1, tile, 0, level)
+        add_parts(send_sum, 0, spread_rows(hot, small(send >> 8), blocks + 2, values))
 
     def step(index, carry):
         each_group(index, stats, fine_count, near, far)
@@ -557,7 +623,7 @@
 
     weight_send = weight_ref[0:LANES, :]
     weight_recv = weight_ref[LANES:, :]
-    odd = odd_ref[0]
+    odd = lax.axis_index("curve") & 1
     to_prev = back(send_sum[0:HB, :], weight_send)
     to_next = back(send_sum[HB + fine_count :, :], weight_send)
     first_ref[...] = jnp.where(odd == 0, to_next, to_prev).astype(BF16)
@@ -570,13 +636,17 @@
     for first in range(0, fine_count, SPAN):
         at = slice(first, first + SPAN)
         moved = slice(HB + first, HB + first + SPAN)
-        term_recv += outer(window[moved, :], recv_sum[at, :])
-        summed_ref[at, :] = (
-            grad_rows[at, :]
-            + back(send_sum[moved, :], weight_send)
-            + back(recv_sum[at, :], weight_recv)
+        received = grad_rows[at, :] * slope_sum[at, :]
+        term_recv += outer(window[moved, :], received)
+        summed = (
+            grad_rows[at, :] + back(send_sum[moved, :], weight_send) + back(received, weight_recv)
         )
-    keep_ref[...] = jnp.where(odd == 0, term_send, term_recv)
+        fine_ref[at, :] = summed.astype(BF16)
+        if first == 0:
+            ends_ref[0] = summed
+        if first == fine_count - SPAN:
+            ends_ref[1] = summed
+    keep_ref[0:LANES, :] = jnp.where(odd == 0, term_send, term_recv)
     gift_ref[...] = jnp.where(odd == 0, term_recv, term_send).astype(BF16)
 
 
@@ -592,26 +662,29 @@
     )
 
 
-def reduced(keep, gift, coarse, device, peers):
-    half = keep.shape[0]
+def reduced(keep, gift, device, peers):
+    half = gift.shape[0]
     odd = (device & 1) == 1
-    own = keep + lax.ppermute(gift, "curve", [(i, i ^ 1) for i in range(peers)]).astype(F32)
+    there = lax.ppermute(gift, "curve", [(i, i ^ 1) for i in range(peers)]).astype(F32)
+    sent = (keep + jnp.pad(there, ((0, keep.shape[0] - half), (0, 0)))).astype(BF16)
+    own, coarse = sent[:half].astype(F32), sent[half:]
     hops = peers // 2
     while hops > 1:
-        rounded = own.astype(BF16)
-        there = lax.ppermute(
-            jnp.concatenate([rounded, coarse], axis=0),
-            "curve",
-            [(i, i ^ hops) for i in range(peers)],
-        )
-        own = rounded.astype(F32) + there[:half].astype(F32)
+        there = lax.ppermute(sent, "curve", [(i, i ^ hops) for i in range(peers)])
+        own = own.astype(BF16).astype(F32) + there[:half].astype(F32)
         coarse = joined((device & hops) != 0, coarse, there[half:])
+        sent = jnp.concatenate([own.astype(BF16), coarse], axis=0)
         hops //= 2
     coarse = coarse.astype(F32)
     there = lax.ppermute(
         jnp.concatenate([own, coarse], axis=0), "curve", [(i, i ^ 1) for i in range(peers)]
     )
-    return joined(odd, own, there[:half]), joined(odd, coarse, there[half:])
+    other, other_coarse = there[:half], there[half:]
+    return (
+        joined(odd, own, other),
+        jnp.where(odd, other_coarse, coarse),
+        jnp.where(odd, coarse, other_coarse),
+    )
 
 
 def per_device(
@@ -630,8 +703,7 @@
 ):
     peers = lax.axis_size("curve")
     device = lax.axis_index("curve")
-    odd = (device & 1).astype(jnp.int32)
-    even = odd == 0
+    even = (device & 1) == 0
     coarse_count = coarse_latent.shape[0]
     fine_count = fine_latent.shape[0]
     edge_count = edge_receivers.shape[0]
@@ -646,7 +718,6 @@
 
     head, end = fine_latent[:HB], fine_latent[fine_count - HB :]
     halos = pair_exchange(jnp.where(even, end, head), jnp.where(even, head, end), peers)
-    parity = odd.reshape(1)
     scalar = pl.BlockSpec(memory_space=pltpu.SMEM)
 
     sent = pl.pallas_call(
@@ -680,33 +751,39 @@
     )
     arrived = lax.all_to_all(sent, "curve", split_axis=0, concat_axis=0, tiled=True)
 
-    slope, window, ordered, stats = pl.pallas_call(
+    pair_count = fine_count // 2
+    in_vmem = pl.BlockSpec(memory_space=pltpu.VMEM)
+    slope, hot, block, window, slope_sum, ordered, stats, slot_hot, slot_block = pl.pallas_call(
         slope_kernel,
         out_shape=(
             jax.ShapeDtypeStruct((edge_count, LANES), F32),
+            jax.ShapeDtypeStruct((edge_count, SPAN), BF16),
+            jax.ShapeDtypeStruct((edge_count, LANES), BF16),
             jax.ShapeDtypeStruct((window_count, LANES), BF16),
+            jax.ShapeDtypeStruct((fine_count, LANES), F32),
             jax.ShapeDtypeStruct((2, edge_rows, LANES), jnp.int32),
             jax.ShapeDtypeStruct((edge_rows, LANES), jnp.int32),
-        ),
-        in_specs=[scalar] + [anywhere] * 6,
-        out_specs=(
-            anywhere,
-            anywhere,
-            pl.BlockSpec(memory_space=pltpu.VMEM),
-            pl.BlockSpec(memory_space=pltpu.VMEM),
-        ),
+            jax.ShapeDtypeStruct((pair_count, SPAN), BF16),
+            jax.ShapeDtypeStruct((pair_count, LANES), jnp.int32),
+        ),
+        in_specs=[anywhere] * 7,
+        out_specs=[anywhere] * 4 + [in_vmem] * 5,
         scratch_shapes=[
             pltpu.VMEM((edge_rows, LANES), jnp.int32),
             pltpu.VMEM((edge_rows, LANES), jnp.int32),
+            pltpu.VMEM((pair_count // LANES, LANES), jnp.int32),
             pltpu.VMEM((window_count, LANES), BF16),
             pltpu.VMEM((2 * LANES, LANES), BF16),
             pltpu.VMEM((2, HB, LANES), BF16),
             pltpu.VMEM((edge_rows, LANES), jnp.int32),
             pltpu.VMEM((edge_count, LANES), F32),
+            pltpu.VMEM((edge_count, SPAN), BF16),
+            pltpu.VMEM((edge_count, LANES), BF16),
             pltpu.SMEM((edge_rows, LANES), jnp.int32),
-            pltpu.SemaphoreType.DMA((6,)),
+            pltpu.SemaphoreType.DMA((7,)),
             pltpu.SemaphoreType.DMA,
-            pltpu.SemaphoreType.DMA((edge_count // TILE + 1,)),
+            pltpu.SemaphoreType.DMA((3, edge_count // TILE)),
+            pltpu.SemaphoreType.DMA,
         ],
         compiler_params=params,
         cost_estimate=pl.CostEstimate(
@@ -714,39 +791,44 @@
         ),
         name="edge_slope",
     )(
-        parity,
         edge_receivers.reshape(-1, LANES),
         edge_offsets.reshape(-1, LANES),
+        pair_slots.reshape(-1, LANES),
         fine_latent,
         edge_weight,
         *halos,
     )
 
-    summed, first, second, keep, gift, coarse_share, term_gain = pl.pallas_call(
-        edge_kernel,
+    coarse_scale = 1.0 / math.sqrt(coarse_count * peers)
+    edge_scale = 1.0 / math.sqrt(edge_count * peers)
+    fine_rows, ends, first, second, keep, gift, term_gain = pl.pallas_call(
+        functools.partial(edge_kernel, coarse_scale),
         out_shape=(
-            jax.ShapeDtypeStruct((fine_count, LANES), F32),
+            jax.ShapeDtypeStruct((fine_count, LANES), BF16),
+            jax.ShapeDtypeStruct((2, HB, LANES), F32),
             jax.ShapeDtypeStruct((HB, LANES), BF16),
             jax.ShapeDtypeStruct((HB, LANES), BF16),
-            jax.ShapeDtypeStruct((LANES, LANES), F32),
+            jax.ShapeDtypeStruct((LANES + share, LANES), F32),
             jax.ShapeDtypeStruct((LANES, LANES), BF16),
-            jax.ShapeDtypeStruct((share, LANES), BF16),
             jax.ShapeDtypeStruct((1, LANES), F32),
         ),
-        in_specs=[scalar] * 2 + [anywhere] * 6,
+        in_specs=[scalar] + [anywhere] * 10,
         scratch_shapes=[
             pltpu.VMEM((SPAN, peers * capacity), BF16),
             pltpu.VMEM((fine_count, LANES), BF16),
             pltpu.VMEM((fine_count, LANES), F32),
             pltpu.VMEM((window_count, LANES), F32),
-            pltpu.VMEM((fine_count, LANES), F32),
             pltpu.VMEM((peers, payload, LANES), BF16),
-            pltpu.VMEM((fine_count // 2 // LANES, LANES), jnp.int32),
+            pltpu.VMEM((pair_count, SPAN), BF16),
+            pltpu.VMEM((pair_count, LANES), jnp.int32),
+            pltpu.VMEM((edge_count, SPAN), BF16),
             pltpu.VMEM((edge_count, LANES), F32),
+            pltpu.VMEM((edge_count, LANES), BF16),
             pltpu.VMEM((2, edge_rows, LANES), jnp.int32),
             pltpu.VMEM((window_count, LANES), BF16),
+            pltpu.VMEM((fine_count, LANES), F32),
             pltpu.VMEM((2 * LANES, LANES), BF16),
-            pltpu.SemaphoreType.DMA((6,)),
+            pltpu.SemaphoreType.DMA((10,)),
         ],
         compiler_params=params,
         cost_estimate=pl.CostEstimate(
@@ -754,34 +836,29 @@
         ),
         name="edge_back",
     )(
-        parity,
         stats,
         arrived,
-        pair_slots.reshape(-1, LANES),
+        slot_hot,
+        slot_block,
+        hot,
         slope,
+        block,
         ordered,
         window,
+        slope_sum,
         edge_weight,
     )
-    edge_terms, coarse_terms = reduced(keep, gift, coarse_share[:chunk], device, peers)
+    edge_terms, term_in, term_out = reduced(keep[: LANES + chunk], gift, device, peers)
     one, two = pair_exchange(first, second, peers)
     from_next, from_prev = jnp.where(even, one, two), jnp.where(even, two, one)
-    coarse_scale = 1.0 / math.sqrt(coarse_count * peers)
-    edge_scale = 1.0 / math.sqrt(edge_count * peers)
-    grad_fine = jnp.concatenate(
-        [
-            summed[:HB] + from_prev.astype(F32),
-            summed[HB : fine_count - HB],
-            summed[fine_count - HB :] + from_next.astype(F32),
-        ],
-        axis=0,
-    ).astype(BF16)
+    grad_fine = fine_rows.at[:HB].set((ends[0] + from_prev.astype(F32)).astype(BF16))
+    grad_fine = grad_fine.at[fine_count - HB :].set((ends[1] + from_next.astype(F32)).astype(BF16))
     return (
         grad_fine,
         edge_terms * edge_scale,
-        coarse_terms[:LANES] * coarse_scale,
-        coarse_terms[LANES:] * coarse_scale,
-        term_gain.reshape(LANES) * coarse_scale,
+        term_in * coarse_scale,
+        term_out * coarse_scale,
+        term_gain.reshape(LANES),
     )
 
 

time: 67.1 us -> 64.4 us (0.960)
  waiting for transfers between devices: 10.3 us -> 7.91 us
  starting transfers between devices: 17.1 us -> 18.9 us
  other arithmetic: 7.61 us -> 6.34 us
  local copies, waits for them, and re-layouts: 1.8 us -> 0.62 us
    scatter x0 -> x2, other arithmetic: none -> 3.13 us  [the longest x1 1.57 us: per_device(): grad_fine.at[fine_count - HB:]]
    pallas_call x1, Pallas kernels: 10.8 us -> 13.5 us  [per_device(): pl.pallas_call(slope_kernel, out_shape=(jax.ShapeDtypeStruct((edge_count,...]
    all_to_all x1, waiting for transfers between devices: 5.21 us -> 2.52 us  [per_device(): lax.all_to_all(sent, 'curve', split_axis=0, concat_axis=0, tiled=True)]
    ppermute x2, starting transfers between devices: 0.59 us -> 2.99 us  [pair_exchange(): lax.ppermute(first, 'curve', pairs)]
    pallas_call x1, Pallas kernels: 6.4 us -> 4.82 us  [per_device(): pl.pallas_call(functools.partial(coarse_kernel, peers), out_shape=jax.Sha...]
    concatenate x4 -> x2, other arithmetic: 1.52 us -> 0.01 us  [reduced(): sent = jnp.concatenate([own.astype(BF16), coarse], axis=0)]
    slice x2 -> x1, local copies, waits for them, and re-layouts: 1.18 us -> 0.01 us  [reduced(): own, coarse = (sent[:half].astype(F32), sent[half:])]
    mul x2 -> x1, other arithmetic: 1.84 us -> 0.67 us  [per_device(): term_out * coarse_scale]
  transfers between devices with their start and end apart: 10 -> 10, of which waited for: 6 -> 5; matrix products, arithmetic and copies ran while one was open for 8% -> 5% of each run, Pallas kernels for 26% -> 29%
where the time goes in v2:
time: 64.4 us; the launch traced here: 63.9 us
  Pallas kernels  29.3 us (45%)
  starting transfers between devices  18.9 us (29%)
  waiting for transfers between devices  7.91 us (12%)
  other arithmetic  6.34 us (10%)
  between operations  0.78 us (1%)
    pallas_call x1, Pallas kernels, per_device(): pl.pallas_call(slope_kernel, out_shape=(jax.ShapeDtypeStruct((edge_count,...  13.5 us
    pallas_call x1, Pallas kernels, per_device(): pl.pallas_call(functools.partial(edge_kernel, coarse_scale), out_shape=(j...  11 us
    all_to_all x1, starting transfers between devices, per_device(): lax.all_to_all(sent, 'curve', split_axis=0, concat_axis=0, tiled=True)  8.27 us
    ppermute x3, starting transfers between devices, reduced(): there = lax.ppermute(sent, 'curve', [(i, i ^ hops) for i in range(peers)])  5.56 us
    pallas_call x1, Pallas kernels, per_device(): pl.pallas_call(functools.partial(coarse_kernel, peers), out_shape=jax.Sha...  4.82 us
    ppermute x3, waiting for transfers between devices, reduced(): there = lax.ppermute(sent, 'curve', [(i, i ^ hops) for i in range(peers)])  3.47 us
    ppermute x2, starting transfers between devices, pair_exchange(): lax.ppermute(first, 'curve', pairs)  2.99 us
    all_to_all x1, waiting for transfers between devices, per_device(): lax.all_to_all(sent, 'curve', split_axis=0, concat_axis=0, tiled=True)  2.52 us
  transfers between devices with their start and end apart: 10, of which 5 were waited for; matrix products, arithmetic and copies ran while one was open for 5% of the time, Pallas kernels for 29%

profile of v2, /device:TPU:0, one launch (start us, length us, event | category | flops | bytes accessed | tf_op | source)
XLA Modules:
  0.0 63.9 jit_solution(10403246945858842083)
XLA Ops:
  0.6 0.9 %broadcast_select_fusion = (bf16[256,128]{1,0:T(8,128)(2,1)S(1)}, bf16[256,128]{1,0:T(8,128)(2,1)S(1)}) fusion(pred[]{:T(512)S(6)} %eq.6, bf16[2048,128]{1,0:T(8,128)(2,1)} %fine_hbm.1), kind=kLoop, calls=%fused_computation.16 | loop fusion | flops 65536 | bytes 262145 | tf_op jit(solution)/shard_map/jit(_where)/select_n | solution.py:720
  1.5 0.5 collective-permute-start
  2.0 1.3 %collective-permute-start.1 = (bf16[256,128]{1,0:T(8,128)(2,1)S(1)}, bf16[256,128]{1,0:T(8,128)(2,1)}, u32[]{:S(2)}, u32[]{:S(2)}) collective-permute-start(bf16[256,128]{1,0:T(8,128)(2,1)S(1)} %get-tuple-element.61), channel_id=1, source_target_pairs={{1,2},{2,1},{3,4},{4,3},{5,6},{6,5},{7,8},{8,7},{9,10},{10,9},{11,... | collective-permute-start | bytes 196616 | tf_op jit(solution)/shard_map/ppermute | solution.py:656
  3.3 4.8 %coarse_block.1 = bf16[16,160,128]{2,1,0:T(8,128)(2,1)} custom-call(bf16[1024,128]{1,0:T(8,128)(2,1)} %latent_ref.1, bf16[1024,128]{1,0:T(8,128)(2,1)} %grad_ref.1, bf16[2,1024]{1,0:T(2,128)(2,1)} %weights_ref.1, s32[16,128]{1,0:T(8,128)} %bitcast.20, bf16[128,128]{1,0:T(8,128)(2,1)} %w_in_ref.1, bf16[128,128]{1,0:T(8,128)(2,1)} %w_out_ref.1, f32[1,128]{1,0:T(1,128)} %bitcast.22), custom_call_target="tpu_custom_call" | custom-call | flops 2000000000 | bytes 2000000 | tf_op jit(solution)/shard_map/coarse_block/pallas_call | solution.py:723
  8.1 8.3 %all-to-all-start = ((bf16[16,160,128]{2,1,0:T(8,128)(2,1)}), bf16[16,160,128]{2,1,0:T(8,128)(2,1)}, u32[]{:S(2)}, u32[]{:S(2)}) async-start(bf16[16,160,128]{2,1,0:T(8,128)(2,1)} %coarse_block.1), calls=%async_computation | async-start | bytes 1310720 | tf_op jit(solution)/shard_map/all_to_all | solution.py:752
  16.5 0.6 copy-done
  17.1 13.5 %edge_slope.1 = (f32[6144,128]{1,0:T(8,128)}, bf16[6144,256]{1,0:T(8,128)(2,1)}, bf16[6144,128]{1,0:T(8,128)(2,1)}, bf16[2560,128]{1,0:T(8,128)(2,1)}, f32[2048,...) custom-call(s32[48,128]{1,0:T(8,128)} %bitcast.18, ...), custom_call_target="tpu_custom_call" | custom-call | flops 16000000000 | bytes 5000000 | tf_op jit(solution)/shard_map/edge_slope/pallas_call | solution.py:756
  30.6 2.5 %all-to-all-done.arrived_hbm = bf16[16,160,128]{2,1,0:T(8,128)(2,1)} async-done(((bf16[16,160,128]{2,1,0:T(8,128)(2,1)}), bf16[16,160,128]{2,1,0:T(8,128)(2,1)}, u32[]{:S(2)}, u32[]{:S(2)}) %all-to-all-start) | async-done | bytes 655392 | tf_op jit(solution)/shard_map/all_to_all | solution.py:752
  33.1 11.0 %edge_back.1 = (bf16[2048,128]{1,0:T(8,128)(2,1)}, f32[2,256,128]{2,1,0:T(8,128)}, bf16[256,128]{1,0:T(8,128)(2,1)}, bf16[256,128]{1,0:T(8,128)(2,1)}, f32[144,1...) custom-call(s32[48,128]{1,0:T(8,128)} %get-tuple-element.45.stats, ...), custom_call_target="tpu_custom_call" | custom-call | flops 24000000000 | bytes 8000000 | tf_op jit(solution)/shard_map/edge_back/pallas_call | solution.py:804
  44.1 0.1 collective-permute-start.4
  44.2 1.4 %collective-permute-done.4 = bf16[128,128]{1,0:T(8,128)(2,1)S(1)} collective-permute-done((bf16[128,128]{1,0:T(8,128)(2,1)}, bf16[128,128]{1,0:T(8,128)(2,1)S(1)}, u32[]{:S(2)}, u32[]{:S(2)}) %collective-permute-start.4) | collective-permute-done | bytes 32800 | tf_op jit(solution)/shard_map/ppermute | solution.py:668
  45.6 0.9 %add_convert_fusion = bf16[144,128]{1,0:T(8,128)(2,1)S(1)} fusion(f32[144,128]{1,0:T(8,128)} %get-tuple-element.58, bf16[128,128]{1,0:T(8,128)(2,1)S(1)} %collective-permute-done.4), kind=kLoop, calls=%fused_computation.8 | loop fusion | flops 55296 | bytes 143360 | tf_op jit(solution)/shard_map/convert_element_type | solution.py:669
  46.5 3.0 %collective-permute-start.5 = (bf16[144,128]{1,0:T(8,128)(2,1)S(1)}, bf16[144,128]{1,0:T(8,128)(2,1)S(1)}, u32[]{:S(2)}, u32[]{:S(2)}) collective-permute-start(bf16[144,128]{1,0:T(8,128)(2,1)S(1)} %add_convert_fusion), channel_id=1, source_target_pairs={{0,8},{1,9},{2,10},{3,11},{4,12},{5,13},{6,14},{7,15},{8,0},{9,1},... | collective-permute-start | bytes 110600 | tf_op jit(solution)/shard_map/ppermute | solution.py:673
  49.5 1.9 %collective-permute-done.5 = bf16[144,128]{1,0:T(8,128)(2,1)S(1)} collective-permute-done((bf16[144,128]{1,0:T(8,128)(2,1)S(1)}, bf16[144,128]{1,0:T(8,128)(2,1)S(1)}, u32[]{:S(2)}, u32[]{:S(2)}) %collective-permute-start.5) | collective-permute-done | bytes 36896 | tf_op jit(solution)/shard_map/ppermute | solution.py:673
  51.4 2.1 %collective-permute-start.6 = (bf16[160,128]{1,0:T(8,128)(2,1)S(1)}, bf16[160,128]{1,0:T(8,128)(2,1)S(1)}, u32[]{:S(2)}, u32[]{:S(2)}) collective-permute-start(bf16[160,128]{1,0:T(8,128)(2,1)S(1)} %pad_maximum_fusion.3), channel_id=1, source_target_pairs={{0,4},{1,5},{2,6},{3,7},{4,0},{5,1},{6,2},{7,3},{8,12},{9,13},{10,... | collective-permute-start | bytes 122888 | tf_op jit(solution)/shard_map/ppermute | solution.py:673
  53.5 0.7 %collective-permute-start.2 = (bf16[256,128]{1,0:T(8,128)(2,1)}, bf16[256,128]{1,0:T(8,128)(2,1)S(1)}, u32[]{:S(2)}, u32[]{:S(2)}) collective-permute-start(bf16[256,128]{1,0:T(8,128)(2,1)} %get-tuple-element.56), channel_id=1, source_target_pairs={{1,2},{2,1},{3,4},{4,3},{5,6},{6,5},{7,8},{8,7},{9,10},{10,9},{11,... | collective-permute-start | bytes 196616 | tf_op jit(solution)/shard_map/ppermute | solution.py:656
  54.1 2.5 %collective-permute-start.3 = (bf16[256,128]{1,0:T(8,128)(2,1)}, bf16[256,128]{1,0:T(8,128)(2,1)S(1)}, u32[]{:S(2)}, u32[]{:S(2)}) collective-permute-start(bf16[256,128]{1,0:T(8,128)(2,1)} %get-tuple-element.57), channel_id=1, source_target_pairs={{0,1},{1,0},{2,3},{3,2},{4,5},{5,4},{6,7},{7,6},{8,9},{9,8},{10,11... | collective-permute-start | bytes 196616 | tf_op jit(solution)/shard_map/ppermute | solution.py:656
  56.7 0.5 collective-permute-start.7
  57.2 0.5 collective-permute-done.3
  57.7 1.6 %fusion.4 = bf16[2048,128]{1,0:T(8,128)(2,1)} fusion(bf16[2048,128]{1,0:T(8,128)(2,1)} %get-tuple-element.54, f32[2,256,128]{2,1,0:T(8,128)} %get-tuple-element.55, bf16[256,128]{1,0:T(8,128)(2,1)S(1)} %collective-permute-done.2, bf16[256,128]{1,0:T(8,128)(2,1)S(1)} %collective-permute-done.3, pred[]{:T(512)S(6)} %eq.6), kind=kLoop, calls=%fused_computation.9 | loop fusion | flops 131072 | bytes 327681 | tf_op jit(solution)/shard_map/scatter | solution.py:854
  59.3 1.5 %collective-permute-done.7 = bf16[192,128]{1,0:T(8,128)(2,1)S(1)} collective-permute-done((bf16[192,128]{1,0:T(8,128)(2,1)S(1)}, bf16[192,128]{1,0:T(8,128)(2,1)S(1)}, u32[]{:S(2)}, u32[]{:S(2)}) %collective-permute-start.7) | collective-permute-done | bytes 49184 | tf_op jit(solution)/shard_map/ppermute | solution.py:673
  61.0 1.6 %fusion.5 = bf16[2048,128]{1,0:T(8,128)(2,1)} fusion(bf16[2048,128]{1,0:T(8,128)(2,1)} %fusion.4, f32[2,256,128]{2,1,0:T(8,128)} %get-tuple-element.55, bf16[256,128]{1,0:T(8,128)(2,1)S(1)} %collective-permute-done.3, bf16[256,128]{1,0:T(8,128)(2,1)S(1)} %collective-permute-done.2, pred[]{:T(512)S(6)} %eq.6), kind=kLoop, calls=%fused_computation.10 | loop fusion | flops 131072 | bytes 327681 | tf_op jit(solution)/shard_map/scatter | solution.py:855
  62.5 0.7 %select_multiply_fusion = (f32[128,128]{1,0:T(8,128)}, f32[128,128]{1,0:T(8,128)}, f32[128,128]{1,0:T(8,128)S(1)}) fusion(f32[256,128]{1,0:T(8,128)S(1)} %collective-permute-done.8, pred[]{:T(512)S(6)} %eq.7, bf16[64,128]{1,0:T(8,128)(2,1)S(1)} %slice.97, bf16[64,128]{1,0:T(8,128)(2,1)S(1)} %maximum_select_fusion.1, pred[]{:T(512)S(6)} %ne.11), kind=kLoop, calls=%fused_computation.11 | loop fusion | flops 229376 | bytes 360450 | tf_op jit(solution)/shard_map/mul | solution.py:860
  63.2 0.7 %fusion.1 = f32[256,128]{1,0:T(8,128)} fusion(f32[128,128]{1,0:T(8,128)S(1)} %convert_add_fusion, f32[128,128]{1,0:T(8,128)S(1)} %get-tuple-element.65, pred[]{:T(512)S(6)} %eq.7), kind=kLoop, calls=%fused_computation.3 | loop fusion | flops 131072 | bytes 262145 | tf_op jit(solution)/shard_map/mul | solution.py:858
  (20 shorter events, 0.2 us)
Async XLA Ops:
  1.5 14.9 %collective-permute-start = (bf16[256,128]{1,0:T(8,128)(2,1)S(1)}, bf16[256,128]{1,0:T(8,128)(2,1)S(1)}, u32[]{:S(2)}, u32[]{:S(2)}) collective-permute-start(bf16[256,128]{1,0:T(8,128)(2,1)S(1)} %get-tuple-element.62), channel_id=1, source_target_pairs={{0,1},{1,0},{2,3},{3,2},{4,5},{5,4},{6,7},{7,6},{8,9},{9,8},{10,11... | collective-permute-start | bytes 196616 | tf_op jit(solution)/shard_map/ppermute | solution.py:656
  2.0 14.4 %collective-permute-start.1 = (bf16[256,128]{1,0:T(8,128)(2,1)S(1)}, bf16[256,128]{1,0:T(8,128)(2,1)}, u32[]{:S(2)}, u32[]{:S(2)}) collective-permute-start(bf16[256,128]{1,0:T(8,128)(2,1)S(1)} %get-tuple-element.61), channel_id=1, source_target_pairs={{1,2},{2,1},{3,4},{4,3},{5,6},{6,5},{7,8},{8,7},{9,10},{10,9},{11,... | collective-permute-start | bytes 196616 | tf_op jit(solution)/shard_map/ppermute | solution.py:656
  8.1 24.9 %all-to-all-start = ((bf16[16,160,128]{2,1,0:T(8,128)(2,1)}), bf16[16,160,128]{2,1,0:T(8,128)(2,1)}, u32[]{:S(2)}, u32[]{:S(2)}) async-start(bf16[16,160,128]{2,1,0:T(8,128)(2,1)} %coarse_block.1), calls=%async_computation | async-start | bytes 1310720 | tf_op jit(solution)/shard_map/all_to_all | solution.py:752
  16.4 0.6 copy-start
  44.1 1.5 %collective-permute-start.4 = (bf16[128,128]{1,0:T(8,128)(2,1)}, bf16[128,128]{1,0:T(8,128)(2,1)S(1)}, u32[]{:S(2)}, u32[]{:S(2)}) collective-permute-start(bf16[128,128]{1,0:T(8,128)(2,1)} %get-tuple-element.59), channel_id=1, source_target_pairs={{0,1},{1,0},{2,3},{3,2},{4,5},{5,4},{6,7},{7,6},{8,9},{9,8},{10,11... | collective-permute-start | bytes 98312 | tf_op jit(solution)/shard_map/ppermute | solution.py:668
  46.5 4.9 %collective-permute-start.5 = (bf16[144,128]{1,0:T(8,128)(2,1)S(1)}, bf16[144,128]{1,0:T(8,128)(2,1)S(1)}, u32[]{:S(2)}, u32[]{:S(2)}) collective-permute-start(bf16[144,128]{1,0:T(8,128)(2,1)S(1)} %add_convert_fusion), channel_id=1, source_target_pairs={{0,8},{1,9},{2,10},{3,11},{4,12},{5,13},{6,14},{7,15},{8,0},{9,1},... | collective-permute-start | bytes 110600 | tf_op jit(solution)/shard_map/ppermute | solution.py:673
  51.4 5.2 %collective-permute-start.6 = (bf16[160,128]{1,0:T(8,128)(2,1)S(1)}, bf16[160,128]{1,0:T(8,128)(2,1)S(1)}, u32[]{:S(2)}, u32[]{:S(2)}) collective-permute-start(bf16[160,128]{1,0:T(8,128)(2,1)S(1)} %pad_maximum_fusion.3), channel_id=1, source_target_pairs={{0,4},{1,5},{2,6},{3,7},{4,0},{5,1},{6,2},{7,3},{8,12},{9,13},{10,... | collective-permute-start | bytes 122888 | tf_op jit(solution)/shard_map/ppermute | solution.py:673
  53.5 3.7 %collective-permute-start.2 = (bf16[256,128]{1,0:T(8,128)(2,1)}, bf16[256,128]{1,0:T(8,128)(2,1)S(1)}, u32[]{:S(2)}, u32[]{:S(2)}) collective-permute-start(bf16[256,128]{1,0:T(8,128)(2,1)} %get-tuple-element.56), channel_id=1, source_target_pairs={{1,2},{2,1},{3,4},{4,3},{5,6},{6,5},{7,8},{8,7},{9,10},{10,9},{11,... | collective-permute-start | bytes 196616 | tf_op jit(solution)/shard_map/ppermute | solution.py:656
  54.1 3.6 %collective-permute-start.3 = (bf16[256,128]{1,0:T(8,128)(2,1)}, bf16[256,128]{1,0:T(8,128)(2,1)S(1)}, u32[]{:S(2)}, u32[]{:S(2)}) collective-permute-start(bf16[256,128]{1,0:T(8,128)(2,1)} %get-tuple-element.57), channel_id=1, source_target_pairs={{0,1},{1,0},{2,3},{3,2},{4,5},{5,4},{6,7},{7,6},{8,9},{9,8},{10,11... | collective-permute-start | bytes 196616 | tf_op jit(solution)/shard_map/ppermute | solution.py:656
  56.7 4.2 %collective-permute-start.7 = (bf16[192,128]{1,0:T(8,128)(2,1)S(1)}, bf16[192,128]{1,0:T(8,128)(2,1)S(1)}, u32[]{:S(2)}, u32[]{:S(2)}) collective-permute-start(bf16[192,128]{1,0:T(8,128)(2,1)S(1)} %pad_maximum_fusion.2), channel_id=1, source_target_pairs={{0,2},{1,3},{2,0},{3,1},{4,6},{5,7},{6,4},{7,5},{8,10},{9,11},{10,... | collective-permute-start | bytes 147464 | tf_op jit(solution)/shard_map/ppermute | solution.py:673
  60.9 1.7 %collective-permute-start.8 = (f32[256,128]{1,0:T(8,128)S(1)}, f32[256,128]{1,0:T(8,128)S(1)}, u32[]{:S(2)}, u32[]{:S(2)}) collective-permute-start(f32[256,128]{1,0:T(8,128)S(1)} %pad_maximum_fusion.1), channel_id=1, source_target_pairs={{0,1},{1,0},{2,3},{3,2},{4,5},{5,4},{6,7},{7,6},{8,9},{9,8},{10,11... | collective-permute-start | bytes 393224 | tf_op jit(solution)/shard_map/ppermute | solution.py:679
